TPU v7x, 32 devices: a whole 2x2x4 slice. The times are simulated.
32 devices in a mesh: dp: 16 (over z, y, x), pipe: 2 (over core).
Axes of the slice: x: 2, y: 2, z: 4, core: 2. Of those that a mesh axis runs over, the one named last changes fastest.
Arguments:
- text_states: bfloat16 [2, 1024, 4096], P('pipe', 'dp')
- image_states: bfloat16 [2, 512, 4096], P(None, ('dp', 'pipe'))
- image_start: int32 [2, 16], P(None, 'dp'), may hold values from 0 to 31
- w_query: bfloat16 [2, 4096, 512], P('pipe')
- w_key: bfloat16 [2, 4096, 128], P('pipe', 'dp')
- w_value: bfloat16 [2, 4096, 128], P('pipe', 'dp'), may hold values from -0.09375 to 0.09375
- w_out: bfloat16 [2, 512, 4096], P('pipe'), may hold values from -0.25 to 0.25
- query_gain: float32 [2, 128], P('pipe'), may hold values from 1 to 2.5
- key_gain: float32 [2, 128], P('pipe'), may hold values from 1 to 2
- cross_gate: float32 [2], P('pipe'), may hold values from 0.3 to 1.2
Outputs:
- final_states: bfloat16 [2, 1024, 4096], P('pipe', 'dp')
All inputs are finite; a program needn't handle non-finite values.
Results may differ from a plain program's by a relative error of at most 0.013.
Values may be sent and summed in bfloat16 or wider, within the bound.
A program may use at most 64 MiB of HBM per device.

v0:
```python
import math

import jax
import jax.numpy as jnp
from jax import lax
from jax.sharding import PartitionSpec as P

epsilon = 1e-06


def shifted(block, axis, distance):
    devices = range(lax.axis_size(axis))
    route = [((i - distance) % len(devices), i) for i in devices]
    return lax.ppermute(block, axis, route)


def normalized(projected, scales):
    mean_square = jnp.mean(projected * projected, axis=-1, keepdims=True)
    return projected * lax.rsqrt(mean_square + epsilon) * scales


def keep_state(current, holding):
    return current


def local(
    text_states,
    image_states,
    image_start,
    w_query,
    w_key,
    w_value,
    w_out,
    query_gain,
    key_gain,
    cross_gate,
):
    sections = lax.axis_size("pipe")
    section_index = lax.axis_index("pipe")
    pictures = lax.all_gather(image_states, "pipe", axis=1, tiled=True)
    batches, image_rows, width = pictures.shape
    flattened = pictures.reshape(batches * image_rows, width)
    head_size = w_key.shape[2]
    head_count = w_query.shape[2] // head_size
    key_full, value_full = (
        lax.all_gather(w_key, "dp", axis=1, tiled=True),
        lax.all_gather(w_value, "dp", axis=1, tiled=True),
    )
    key_sums = jnp.dot(flattened, key_full[0], preferred_element_type=jnp.float32)
    value_sums = jnp.dot(flattened, value_full[0], preferred_element_type=jnp.float32)
    key_rows = (
        normalized(key_sums, key_gain[0])
        .astype(jnp.bfloat16)
        .reshape(batches, image_rows, head_size)
    )
    value_rows = value_sums.astype(jnp.bfloat16).reshape(batches, image_rows, head_size)
    query_weight = w_query[0]
    out_weight = w_out[0]
    factor = jnp.tanh(cross_gate[0])
    tok_rows = text_states.shape[1]
    positions = jnp.arange(tok_rows, dtype=jnp.int32)
    root_size = math.sqrt(head_size)

    def apply_layer(current, holding):
        own_keys = lax.dynamic_index_in_dim(key_rows, holding, 0, keepdims=False)
        own_values = lax.dynamic_index_in_dim(value_rows, holding, 0, keepdims=False)
        query_sums = jnp.dot(current, query_weight, preferred_element_type=jnp.float32)
        query_sums = query_sums.reshape(tok_rows * head_count, head_size)
        queries = normalized(query_sums, query_gain[0]).astype(jnp.bfloat16)
        scores = jnp.dot(queries, own_keys.T, preferred_element_type=jnp.float32) / root_size
        exponent = jnp.exp(scores)
        probs = (exponent / jnp.sum(exponent, axis=-1, keepdims=True)).astype(jnp.bfloat16)
        attended = jnp.dot(probs, own_values, preferred_element_type=jnp.float32).astype(
            jnp.bfloat16
        )
        attended = attended.reshape(tok_rows, head_count * head_size)
        update = jnp.dot(attended, out_weight, preferred_element_type=jnp.float32)
        first_seen = lax.dynamic_index_in_dim(image_start[:, 0], holding, 0, keepdims=False)
        seen = (positions >= first_seen).astype(jnp.float32)[:, None]
        return (current.astype(jnp.float32) + factor * seen * update).astype(jnp.bfloat16)

    current = text_states[0]
    for moment in range(sections):
        holding = jnp.mod(section_index - moment, sections)
        current = lax.cond(moment <= section_index, apply_layer, keep_state, current, holding)
        current = shifted(current, "pipe", 1)
    return current[None]


def solution(mesh):
    placed = (
        P("pipe", "dp", None),
        P(None, ("dp", "pipe"), None),
        P(None, "dp"),
        P("pipe", None, None),
        P("pipe", "dp", None),
        P("pipe", "dp", None),
        P("pipe", None, None),
        P("pipe", None),
        P("pipe", None),
        P("pipe"),
    )
    return jax.shard_map(
        local, mesh=mesh, in_specs=placed, out_specs=P("pipe", "dp", None), check_vma=False
    )
```

profile of v0, /device:TPU:0, one launch (start us, length us, event | category | flops | bytes accessed | tf_op | source)
XLA Modules:
  0.0 154.6 jit_solution(941540045320361271)
XLA Ops:
  6.5 0.0 copy-start
  6.5 0.0 copy-start.2
  6.5 0.0 copy-start.1
  6.5 0.0 all-gather.3.cloned.1.call-start
  6.5 0.7 all-gather.3.cloned.1.call-update
  7.3 0.0 all-gather.5.cloned.1.call-start
  7.3 0.7 all-gather.5.cloned.1.call-update
  8.7 2.5 %all_gather.9 = bf16[2,32,4096]{2,1,0:T(8,128)(2,1)S(1)} all-gather(bf16[2,16,4096]{2,1,0:T(8,128)(2,1)} %param.15), channel_id=1, replica_groups=mesh['dp'=16,'pipe'=2] {'pipe'}, dimensions={1}, use_global_device_ids=true | all-gather | bytes 786432 | tf_op jit(solution)/shard_map/all_gather | solution.py:40
  11.2 57.0 %all-gather.3.cloned.1.call-done = bf16[1,4096,128]{2,1,0:T(8,128)(2,1)} async-done(((bf16[1,256,128]{2,1,0:T(8,128)(2,1)}), bf16[1,4096,128]{2,1,0:T(8,128)(2,1)}) %all-gather.3.cloned.1.call-update) | async-done | bytes 1048592 | tf_op jit(solution)/shard_map/all_gather | solution.py:46
  68.1 1.6 %multiply_reduce_fusion = (f32[64]{0:T(128)S(1)}, f32[64,128]{1,0:T(8,128)S(1)}) fusion(bf16[64,4096]{1,0:T(8,128)(2,1)S(1)} %bitcast.71, bf16[1,4096,128]{2,1,0:T(8,128)(2,1)} %all-gather.3.cloned.1.call-done), kind=kOutput, calls=%fused_computation.47 | convolution fusion | flops 67125184 | bytes 1605888 | tf_op jit(solution)/shard_map/dot_general | solution.py:49
  69.8 0.7 multiply_convert_fusion
  70.5 54.5 %all-gather.5.cloned.1.call-done = bf16[1,4096,128]{2,1,0:T(8,128)(2,1)} async-done(((bf16[1,256,128]{2,1,0:T(8,128)(2,1)}), bf16[1,4096,128]{2,1,0:T(8,128)(2,1)}) %all-gather.5.cloned.1.call-update) | async-done | bytes 1048592 | tf_op jit(solution)/shard_map/all_gather | solution.py:47
  125.0 1.5 convolution_convert_fusion.2
  126.5 0.0 copy-done
  126.6 0.0 copy-done.2
  126.6 0.0 copy-done.1
  126.6 8.2 %conditional.2 = (bf16[64,4096]{1,0:T(8,128)(2,1)S(1)}) conditional(s32[]{:T(128)} %convert_element_type.71, bf16[64,4096]{1,0:T(8,128)(2,1)S(1)} %bitcast.73, (bf16[64,4096]{1,0:T(8,128)(2,1)S(1)}, s32[]{:T(128)}, s32[2,1]{0,1:T(1,128)S(1)}, s32[64]{0:T(128)S(1)}, f32[]{:T(128)}, /*index=5*/bf16[4096,512]{1,0:T(8,128)(2,1)}, f32[1,128]{1,0:T(1,128)S(1)}, ...), branch_computations={%region_1.2_spmd, %region_2.5_spmd} | conditional | flops 542343296 | bytes 11630007 | solution.py:85
  126.6 3.0 %fusion.27 = (f32[64,512]{1,0:T(8,128)S(1)}, f32[64,512]{1,0:T(8,128)S(1)}) fusion(bf16[64,4096]{1,0:T(8,128)(2,1)S(1)} %get-tuple-element.217, bf16[4096,512]{1,0:T(8,128)(2,1)} %get-tuple-element.222), kind=kOutput, calls=%fused_computation.49 | convolution fusion | flops 268468224 | bytes 4980736 | tf_op jit(solution)/shard_map/cond/branch_1_fun/dot_general | solution.py:67
  129.7 0.1 reduce_sum.48
  129.8 0.1 rsqrt.30
  129.9 0.1 mul.110
  130.1 0.1 convert_element_type.56
  130.1 0.2 fusion.28
  130.3 0.2 convolution_convert_fusion
  130.5 0.1 reshape.97
  130.6 0.6 constant_dynamic-slice_fusion
  131.1 0.6 compare_select_fusion
  131.7 3.1 %fusion.1 = bf16[64,4096]{1,0:T(8,128)(2,1)S(1)} fusion(bf16[64,512]{1,0:T(8,128)(2,1)S(1)} %reshape.97, bf16[512,4096]{1,0:T(8,128)(2,1)} %get-tuple-element.226, bf16[64,4096]{1,0:T(8,128)(2,1)S(1)} %get-tuple-element.217, f32[64]{0:T(128)S(1)} %compare_select_fusion), kind=kOutput, calls=%fused_computation.2 | convolution fusion | flops 269484032 | bytes 5308672 | tf_op jit(solution)/shard_map/cond/branch_1_fun/dot_general | solution.py:77
  134.8 0.1 collective-permute-start
  134.9 1.9 %collective-permute-done = bf16[64,4096]{1,0:T(8,128)(2,1)S(1)} collective-permute-done((bf16[64,4096]{1,0:T(8,128)(2,1)S(1)}, bf16[64,4096]{1,0:T(8,128)(2,1)S(1)}, u32[]{:S(2)}, u32[]{:S(2)}) %collective-permute-start) | collective-permute-done | bytes 524320 | tf_op jit(solution)/shard_map/ppermute | solution.py:14
  136.8 8.6 %collective-permute-start.1 = (bf16[64,4096]{1,0:T(8,128)(2,1)S(1)}, bf16[64,4096]{1,0:T(8,128)(2,1)S(1)}, u32[]{:S(2)}, u32[]{:S(2)}) collective-permute-start(bf16[64,4096]{1,0:T(8,128)(2,1)S(1)} %get-tuple-element.270), channel_id=1, source_target_pairs={{1,0},{0,1},{3,2},{2,3},{5,4},{4,5},{7,6},{6,7},{9,8},{8,9},{11,10... | collective-permute-start | bytes 1572872 | tf_op jit(solution)/shard_map/ppermute | solution.py:14
  145.4 1.5 collective-permute-done.1
  147.0 0.8 copy.23
  (8 shorter events, 0.1 us)
Async XLA Ops:
  6.5 120.0 %copy-start = (bf16[1,64,4096]{2,1,0:T(8,128)(2,1)S(1)}, bf16[1,64,4096]{2,1,0:T(8,128)(2,1)}, u32[]{:S(2)}) copy-start(bf16[1,64,4096]{2,1,0:T(8,128)(2,1)} %param.14) | copy-start | bytes 1572868
  6.5 120.0 %copy-start.2 = (s32[2,1]{0,1:T(1,128)S(1)}, s32[2,1]{0,1:T(1,128)}, u32[]{:S(2)}) copy-start(s32[2,1]{0,1:T(1,128)} %param.16) | copy-start | bytes 28
  6.5 120.0 %copy-start.1 = (f32[1,128]{1,0:T(1,128)S(1)}, f32[1,128]{1,0:T(1,128)}, u32[]{:S(2)}) copy-start(f32[1,128]{1,0:T(1,128)} %param.21) | copy-start | bytes 1540
  6.5 61.6 %all-gather.3.cloned.1.call-start = ((), (), s32[]{:S(2)}) async-start(), calls=%async_computation | async-start | bytes 1114112 | tf_op jit(solution)/shard_map/all_gather | solution.py:46
  7.3 117.7 %all-gather.5.cloned.1.call-start = ((), (), s32[]{:S(2)}) async-start(), calls=%async_computation.1 | async-start | bytes 1114112 | tf_op jit(solution)/shard_map/all_gather | solution.py:47
  134.8 2.0 %collective-permute-start = (bf16[64,4096]{1,0:T(8,128)(2,1)S(1)}, bf16[64,4096]{1,0:T(8,128)(2,1)S(1)}, u32[]{:S(2)}, u32[]{:S(2)}) collective-permute-start(bf16[64,4096]{1,0:T(8,128)(2,1)S(1)} %get-tuple-element.269), channel_id=1, source_target_pairs={{1,0},{0,1},{3,2},{2,3},{5,4},{4,5},{7,6},{6,7},{9,8},{8,9},{11,10... | collective-permute-start | bytes 1572872 | tf_op jit(solution)/shard_map/ppermute | solution.py:14
  136.8 10.2 %collective-permute-start.1 = (bf16[64,4096]{1,0:T(8,128)(2,1)S(1)}, bf16[64,4096]{1,0:T(8,128)(2,1)S(1)}, u32[]{:S(2)}, u32[]{:S(2)}) collective-permute-start(bf16[64,4096]{1,0:T(8,128)(2,1)S(1)} %get-tuple-element.270), channel_id=1, source_target_pairs={{1,0},{0,1},{3,2},{2,3},{5,4},{4,5},{7,6},{6,7},{9,8},{8,9},{11,10... | collective-permute-start | bytes 1572872 | tf_op jit(solution)/shard_map/ppermute | solution.py:14
Sparse Core Ops, SparseCore 0:
  10.1 57.9 all-gather.2
  70.9 54.0 all-gather.4
where the time goes:
time: 155 us
  waiting for transfers between devices  116 us (75%)
  between operations  14.2 us (9%)
  matrix products  9.68 us (6%)
  starting transfers between devices  8.74 us (6%)
  blocking collectives  2.47 us (2%)
  local copies, waits for them, and re-layouts  1.73 us (1%)
    all_gather x1, waiting for transfers between devices, local(): lax.all_gather(w_key, 'dp', axis=1, tiled=True)  57 us
    all_gather x1, waiting for transfers between devices, local(): lax.all_gather(w_value, 'dp', axis=1, tiled=True)  54.5 us
    ppermute x2, starting transfers between devices, shifted(): return lax.ppermute(block, axis, route)  8.7 us
    ppermute x2, waiting for transfers between devices, shifted(): return lax.ppermute(block, axis, route)  3.43 us
  transfers between devices with their start and end apart: 4, of which 4 were waited for; matrix products, arithmetic and copies ran while one was open for 2% of the time, Pallas kernels for 0%

commit v1 on v0

--- a/solution.py
+++ b/solution.py
@@ -1,11 +1,17 @@
+import functools
 import math
 
 import jax
 import jax.numpy as jnp
 from jax import lax
+from jax.experimental import pallas as pl
+from jax.experimental.pallas import tpu as pltpu
 from jax.sharding import PartitionSpec as P
 
 epsilon = 1e-06
+MESH = pl.DeviceIdType.MESH
+QUAD = 4
+PIECES = 4
 
 
 def shifted(block, axis, distance):
@@ -87,6 +93,374 @@
     return current[None]
 
 
+def kernel(
+    lines,
+    text_ref,
+    image_ref,
+    start_ref,
+    wq_ref,
+    wk_ref,
+    wv_ref,
+    wo_ref,
+    qg_ref,
+    kg_ref,
+    gate_ref,
+    out_ref,
+    text_v,
+    wq_v,
+    wo_v,
+    wkv,
+    img,
+    part,
+    part_out,
+    part_in,
+    query_v,
+    small,
+    load_sem,
+    w_send,
+    w_recv,
+    i_send,
+    i_recv,
+    relay_send,
+    relay_recv,
+    big_send,
+    big_recv,
+    small_send,
+    small_recv,
+    p_send,
+    p_recv,
+):
+    place = lax.axis_index("dp")
+    core = lax.axis_index("pipe")
+    other = 1 - core
+    line = place // QUAD
+    spot = place % QUAD
+    depth = wk_ref.shape[1]
+    head = wk_ref.shape[2]
+    tokens, width = text_v.shape
+    heads = wq_ref.shape[2] // head
+    image_rows = image_ref.shape[1]
+    span = QUAD * depth
+
+    def quad_peer(distance):
+        return line * QUAD + (spot + distance) % QUAD
+
+    def line_peer(distance):
+        return ((line + distance) % lines) * QUAD + spot
+
+    def rows_of(index):
+        return pl.ds(pl.multiple_of(index * depth, depth), depth)
+
+    loads = [
+        pltpu.make_async_copy(wk_ref.at[0], wkv.at[0, rows_of(spot), pl.ds(0, head)], load_sem.at[0]),
+        pltpu.make_async_copy(wv_ref.at[0], wkv.at[0, rows_of(spot), pl.ds(head, head)], load_sem.at[1]),
+        pltpu.make_async_copy(
+            image_ref.at[core, :, pl.ds(pl.multiple_of(line * span, span), span)],
+            img.at[line, pl.ds(pl.multiple_of(core * image_rows, image_rows), image_rows)],
+            load_sem.at[2],
+        ),
+        pltpu.make_async_copy(text_ref.at[0], text_v, load_sem.at[3]),
+        pltpu.make_async_copy(wq_ref.at[0], wq_v.at[0], load_sem.at[4]),
+        pltpu.make_async_copy(wo_ref.at[0], wo_v.at[0], load_sem.at[5]),
+    ]
+    for load in loads:
+        load.start()
+
+    barrier = pltpu.get_barrier_semaphore()
+    peers = [(quad_peer(d), core) for d in range(1, QUAD)]
+    peers += [(line_peer(d), side) for d in range(1, lines) for side in (core, other)]
+    peers += [(place, other)]
+    for peer in peers:
+        pl.semaphore_signal(barrier, inc=1, device_id=peer, device_id_type=MESH)
+    pl.semaphore_wait(barrier, len(peers))
+
+    image_copies = []
+    for distance in range(lines):
+        target = (line + distance) % lines
+        columns = pl.ds(pl.multiple_of(target * span, span), span)
+        for turn in range(2):
+            if distance == 0 and turn == 0:
+                continue
+            side = core if turn == 0 else other
+            copy = pltpu.make_async_remote_copy(
+                src_ref=image_ref.at[side, :, columns],
+                dst_ref=img.at[line, pl.ds(pl.multiple_of(core * image_rows, image_rows), image_rows)],
+                send_sem=i_send.at[distance, turn],
+                recv_sem=i_recv.at[distance, turn],
+                device_id=(line_peer(distance), side),
+                device_id_type=MESH,
+            )
+            copy.start()
+            image_copies.append(copy)
+
+    weight_copies = []
+    for distance in range(1, QUAD):
+        for which, ref in enumerate((wk_ref, wv_ref)):
+            copy = pltpu.make_async_remote_copy(
+                src_ref=ref.at[0],
+                dst_ref=wkv.at[0, rows_of(spot), pl.ds(which * head, head)],
+                send_sem=w_send.at[distance, which],
+                recv_sem=w_recv.at[distance, which],
+                device_id=(quad_peer(distance), core),
+                device_id_type=MESH,
+            )
+            copy.start()
+            weight_copies.append(copy)
+
+    def across(src, dst, send, recv):
+        return pltpu.make_async_remote_copy(
+            src_ref=src,
+            dst_ref=dst,
+            send_sem=send,
+            recv_sem=recv,
+            device_id=(place, other),
+            device_id_type=MESH,
+        )
+
+    query_rows = width // PIECES
+    out_rows = wo_ref.shape[1] // PIECES
+    query_pieces = [
+        across(
+            wq_ref.at[0, pl.ds(i * query_rows, query_rows)],
+            wq_v.at[1, pl.ds(i * query_rows, query_rows)],
+            big_send.at[0, i],
+            big_recv.at[0, i],
+        )
+        for i in range(PIECES)
+    ]
+    out_pieces = [
+        across(
+            wo_ref.at[0, pl.ds(i * out_rows, out_rows)],
+            wo_v.at[1, pl.ds(i * out_rows, out_rows)],
+            big_send.at[1, i],
+            big_recv.at[1, i],
+        )
+        for i in range(PIECES)
+    ]
+    small_copy = across(small.at[0], small.at[1], small_send, small_recv)
+
+    def relay(distance):
+        rows = rows_of((spot + QUAD - distance) % QUAD)
+        return across(wkv.at[0, rows], wkv.at[1, rows], relay_send.at[distance], relay_recv.at[distance])
+
+    small[0, 0:1] = qg_ref[...]
+    small[0, 1:2] = kg_ref[...]
+    small[0, 2:3] = jnp.full((1, head), gate_ref[0], jnp.float32)
+
+    loads[0].wait()
+    loads[1].wait()
+
+    @pl.when(core == 1)
+    def _():
+        small_copy.start()
+        relay(0).start()
+        for piece in query_pieces:
+            piece.start()
+        for distance in range(1, QUAD):
+            weight_copies[2 * distance - 2].wait_recv()
+            weight_copies[2 * distance - 1].wait_recv()
+            relay(distance).start()
+        for piece in out_pieces:
+            piece.start()
+
+    chunk = 512
+
+    def project(source, slot):
+        steps = width // chunk
+
+        def step(i, total):
+            at = pl.ds(pl.multiple_of(i * chunk, chunk), chunk)
+            return total + jnp.dot(source[:, at], wq_v[slot, at, :], preferred_element_type=jnp.float32)
+
+        sums = lax.fori_loop(0, steps, step, jnp.zeros((tokens, heads * head), jnp.float32))
+        for h in range(heads):
+            query_v[h * tokens : (h + 1) * tokens, :] = normalized(
+                sums[:, h * head : (h + 1) * head], small[slot, 0:1]
+            ).astype(jnp.bfloat16)
+
+    loads[3].wait()
+    loads[4].wait()
+    project(text_v, 0)
+
+    loads[2].wait()
+    for copy in image_copies:
+        copy.wait_recv()
+
+    def partial_sums(slot):
+        groups = 2 * image_rows
+        sums = jnp.dot(
+            img[...].reshape(lines * groups, span), wkv[slot], preferred_element_type=jnp.float32
+        )
+        sums = sums.reshape(lines, groups, 2 * head)
+        part[:, slot] = sums
+        part_out[:, slot] = sums.astype(jnp.bfloat16)
+
+    def partial_copy(slot, distance):
+        return pltpu.make_async_remote_copy(
+            src_ref=part_out.at[(line + distance) % lines, slot],
+            dst_ref=part_in.at[line, slot],
+            send_sem=p_send.at[slot, distance],
+            recv_sem=p_recv.at[slot, distance],
+            device_id=(line_peer(distance), core),
+            device_id_type=MESH,
+        )
+
+    @pl.when(core == 0)
+    def _():
+        for copy in weight_copies:
+            copy.wait_recv()
+
+    partial_sums(0)
+    for distance in range(1, lines):
+        partial_copy(0, distance).start()
+
+    @pl.when(core == 0)
+    def _():
+        for distance in range(QUAD):
+            relay(distance).wait_recv()
+        partial_sums(1)
+        for distance in range(1, lines):
+            partial_copy(1, distance).start()
+
+    positions = lax.broadcasted_iota(jnp.int32, (tokens, chunk), 0)
+    seen = (positions >= start_ref[core, 0]).astype(jnp.float32)
+    root_size = math.sqrt(head)
+
+    def attend(source, slot, ready):
+        total = part[line, slot]
+        for distance in range(1, lines):
+            partial_copy(slot, distance).wait_recv()
+            total += part_in[(line + lines - distance) % lines, slot].astype(jnp.float32)
+        keys = normalized(total[:, :head], small[slot, 1:2]).astype(jnp.bfloat16)
+        values = total[:, head:].astype(jnp.bfloat16)
+        scores = (
+            lax.dot_general(
+                query_v[...], keys, (((1,), (1,)), ((), ())), preferred_element_type=jnp.float32
+            )
+            / root_size
+        )
+        exponent = jnp.exp(scores)
+        probs = (exponent / jnp.sum(exponent, axis=-1, keepdims=True)).astype(jnp.bfloat16)
+        attended = jnp.dot(probs, values, preferred_element_type=jnp.float32).astype(jnp.bfloat16)
+        attended = jnp.concatenate(
+            [attended[h * tokens : (h + 1) * tokens] for h in range(heads)], axis=1
+        )
+        factor = jnp.tanh(small[slot, 2:3])[:, 0:1] * seen
+        ready()
+
+        def step(i, carry):
+            at = pl.ds(pl.multiple_of(i * chunk, chunk), chunk)
+            update = jnp.dot(attended, wo_v[slot, :, at], preferred_element_type=jnp.float32)
+            out_ref[0, :, at] = (source(at).astype(jnp.float32) + factor * update).astype(jnp.bfloat16)
+            return carry
+
+        lax.fori_loop(0, width // chunk, step, 0)
+
+    attend(lambda at: text_v[:, at], 0, loads[5].wait)
+
+    @pl.when(core == 0)
+    def _():
+        small_copy.wait_recv()
+        for piece in query_pieces:
+            piece.wait_recv()
+        project(out_ref.at[0], 1)
+
+        def ready():
+            for piece in out_pieces:
+                piece.wait_recv()
+
+        attend(lambda at: out_ref[0, :, at], 1, ready)
+
+    for copy in image_copies + weight_copies:
+        copy.wait_send()
+    for distance in range(1, lines):
+        partial_copy(0, distance).wait_send()
+
+    @pl.when(core == 0)
+    def _():
+        for distance in range(1, lines):
+            partial_copy(1, distance).wait_send()
+
+    @pl.when(core == 1)
+    def _():
+        small_copy.wait_send()
+        for distance in range(QUAD):
+            relay(distance).wait_send()
+        for piece in query_pieces + out_pieces:
+            piece.wait_send()
+
+
+def local_fused(
+    text_states,
+    image_states,
+    image_start,
+    w_query,
+    w_key,
+    w_value,
+    w_out,
+    query_gain,
+    key_gain,
+    cross_gate,
+):
+    lines = lax.axis_size("dp") // QUAD
+    tokens, width = text_states.shape[1:]
+    image_rows = image_states.shape[1]
+    depth, head = w_key.shape[1:]
+    columns = w_query.shape[2]
+    heads = columns // head
+    span = QUAD * depth
+    groups = 2 * image_rows
+    anywhere = pl.BlockSpec(memory_space=pl.ANY)
+    vmem = pl.BlockSpec(memory_space=pltpu.VMEM)
+    smem = pl.BlockSpec(memory_space=pltpu.SMEM)
+    dma = pltpu.SemaphoreType.DMA
+    return pl.pallas_call(
+        functools.partial(kernel, lines),
+        out_shape=jax.ShapeDtypeStruct((1, tokens, width), jnp.bfloat16),
+        in_specs=[anywhere, anywhere, smem, anywhere, anywhere, anywhere, anywhere, vmem, vmem, smem],
+        out_specs=vmem,
+        scratch_shapes=[
+            pltpu.VMEM((tokens, width), jnp.bfloat16),
+            pltpu.VMEM((2, width, columns), jnp.bfloat16),
+            pltpu.VMEM((2, columns, width), jnp.bfloat16),
+            pltpu.VMEM((2, span, 2 * head), jnp.bfloat16),
+            pltpu.VMEM((lines, groups, span), jnp.bfloat16),
+            pltpu.VMEM((lines, 2, groups, 2 * head), jnp.float32),
+            pltpu.VMEM((lines, 2, groups, 2 * head), jnp.bfloat16),
+            pltpu.VMEM((lines, 2, groups, 2 * head), jnp.bfloat16),
+            pltpu.VMEM((heads * tokens, head), jnp.bfloat16),
+            pltpu.VMEM((2, 8, head), jnp.float32),
+            dma((6,)),
+            dma((QUAD, 2)),
+            dma((QUAD, 2)),
+            dma((lines, 2)),
+            dma((lines, 2)),
+            dma((QUAD,)),
+            dma((QUAD,)),
+            dma((2, PIECES)),
+            dma((2, PIECES)),
+            dma,
+            dma,
+            dma((2, lines)),
+            dma((2, lines)),
+        ],
+        compiler_params=pltpu.CompilerParams(
+            collective_id=0, has_side_effects=True, vmem_limit_bytes=48 * 2**20
+        ),
+    )(
+        text_states,
+        image_states,
+        image_start,
+        w_query,
+        w_key,
+        w_value,
+        w_out,
+        query_gain,
+        key_gain,
+        cross_gate,
+    )
+
+
 def solution(mesh):
     placed = (
         P("pipe", "dp", None),
@@ -100,6 +474,11 @@
         P("pipe", None),
         P("pipe"),
     )
+    fits = mesh.shape["pipe"] == 2 and mesh.shape["dp"] == QUAD * QUAD
     return jax.shard_map(
-        local, mesh=mesh, in_specs=placed, out_specs=P("pipe", "dp", None), check_vma=False
+        local_fused if fits else local,
+        mesh=mesh,
+        in_specs=placed,
+        out_specs=P("pipe", "dp", None),
+        check_vma=False,
     )

time: 155 us -> 33.8 us (0.22)
  waiting for transfers between devices: 116 us -> 0 us
  Pallas kernels: 0 us -> 24.1 us
  between operations: 14.2 us -> 0.67 us
  matrix products: 9.68 us -> 0 us
  starting transfers between devices: 8.74 us -> 0 us
  local copies, waits for them, and re-layouts: 1.73 us -> 8.7 us
  blocking collectives: 2.47 us -> 0 us
    all_gather x2 -> x0, waiting for transfers between devices: 111 us -> none  [the longest x1 57 us: local(): lax.all_gather(w_key, 'dp', axis=1, tiled=True)]
    pallas_call x0 -> x1, Pallas kernels: none -> 24.1 us  [local_fused(): pl.pallas_call(functools.partial(kernel, lines), out_shape=jax.ShapeDtype...]
    dot_general x6 -> x0, matrix products: 9.68 us -> none  [the longest x1 3.1 us: apply_layer(): update = jnp.dot(attended, out_weight, preferred_element_type=jnp.float32)]
    ppermute x2 -> x0, starting transfers between devices: 8.7 us -> none  [shifted(): return lax.ppermute(block, axis, route)]
    unnamed x7 -> x16, local copies, waits for them, and re-layouts: 0.8 us -> 8.7 us
    ppermute x2 -> x0, waiting for transfers between devices: 3.43 us -> none  [shifted(): return lax.ppermute(block, axis, route)]
    all_gather x1 -> x0, blocking collectives: 2.47 us -> none  [local(): pictures = lax.all_gather(image_states, 'pipe', axis=1, tiled=True)]
  transfers between devices with their start and end apart: 4 -> 0, of which waited for: 4 -> 0; matrix products, arithmetic and copies ran while one was open for 2% -> 0% of each run, Pallas kernels for 0% -> 0%
where the time goes in v1:
time: 33.8 us; the launch traced here: 33.4 us
  Pallas kernels  24.1 us (71%)
  local copies, waits for them, and re-layouts  8.7 us (26%)
  between operations  0.67 us (2%)
    pallas_call x1, Pallas kernels, local_fused(): pl.pallas_call(functools.partial(kernel, lines), out_shape=jax.ShapeDtype...  24.1 us
    unnamed x16, local copies, waits for them, and re-layouts  8.7 us

profile of v1, /device:TPU:0, one launch (start us, length us, event | category | flops | bytes accessed | tf_op | source)
XLA Modules:
  0.0 33.4 jit_solution(18426885755052864012)
XLA Ops:
  0.7 0.7 %copy.11.start_ref = s32[2,1]{1,0:T(2,128)S(1)} copy(s32[2,1]{0,1:T(1,128)} %param.12) | data formatting | bytes 16 | tf_op args[2]
  1.4 0.0 copy-start
  1.4 2.2 %copy-done = bf16[1,4096,512]{2,1,0:T(8,128)(2,1)S(1)} copy-done((bf16[1,4096,512]{2,1,0:T(8,128)(2,1)S(1)}, bf16[1,4096,512]{2,1,0:T(8,128)(2,1)}, u32[]{:S(2)}) %copy-start) | copy-done | bytes 4194328
  3.6 0.0 copy-start.1
  3.6 1.0 %copy-done.1 = bf16[1,64,4096]{2,1,0:T(8,128)(2,1)S(1)} copy-done((bf16[1,64,4096]{2,1,0:T(8,128)(2,1)S(1)}, bf16[1,64,4096]{2,1,0:T(8,128)(2,1)}, u32[]{:S(2)}) %copy-start.1) | copy-done | bytes 524312
  4.6 0.0 copy-start.2
  4.6 0.9 %copy-done.2 = bf16[2,16,4096]{2,1,0:T(8,128)(2,1)S(1)} copy-done((bf16[2,16,4096]{2,1,0:T(8,128)(2,1)S(1)}, bf16[2,16,4096]{2,1,0:T(8,128)(2,1)}, u32[]{:S(2)}) %copy-start.2) | copy-done | bytes 262168
  5.6 0.0 copy-start.3
  5.6 0.8 %copy-done.3 = bf16[1,256,128]{2,1,0:T(8,128)(2,1)S(1)} copy-done((bf16[1,256,128]{2,1,0:T(8,128)(2,1)S(1)}, bf16[1,256,128]{2,1,0:T(8,128)(2,1)}, u32[]{:S(2)}) %copy-start.3) | copy-done | bytes 65560
  6.4 0.0 copy-start.4
  6.4 0.8 %copy-done.4 = bf16[1,256,128]{2,1,0:T(8,128)(2,1)S(1)} copy-done((bf16[1,256,128]{2,1,0:T(8,128)(2,1)S(1)}, bf16[1,256,128]{2,1,0:T(8,128)(2,1)}, u32[]{:S(2)}) %copy-start.4) | copy-done | bytes 65560
  7.3 0.0 copy-start.5
  7.3 0.7 %copy-done.5 = f32[1,128]{1,0:T(1,128)S(1)} copy-done((f32[1,128]{1,0:T(1,128)S(1)}, f32[1,128]{1,0:T(1,128)}, u32[]{:S(2)}) %copy-start.5) | copy-done | bytes 536
  7.9 0.0 copy-start.6
  7.9 0.7 %copy-done.6 = f32[1,128]{1,0:T(1,128)S(1)} copy-done((f32[1,128]{1,0:T(1,128)S(1)}, f32[1,128]{1,0:T(1,128)}, u32[]{:S(2)}) %copy-start.6) | copy-done | bytes 536
  8.6 24.1 %shard_map.100 = bf16[1,64,4096]{2,1,0:T(8,128)(2,1)S(1)} custom-call(bf16[1,64,4096]{2,1,0:T(8,128)(2,1)S(1)} %copy-done.1, bf16[2,16,4096]{2,1,0:T(8,128)(2,1)S(1)} %copy-done.2, s32[2,1]{1,0:T(2,128)S(1)} %copy.11.start_ref, bf16[1,4096,512]{2,1,0:T(8,128)(2,1)S(1)} %copy-done, bf16[1,256,128]{2,1,0:T(8,128)(2,1)S(1)} %copy-done.3, ...), custom_call_target="tpu_custom_call" | custom-call | tf_op jit(solution)/shard_map/pallas_call | solution.py:417
  32.6 0.8 %copy.14 = bf16[1,64,4096]{2,1,0:T(8,128)(2,1)} copy(bf16[1,64,4096]{2,1,0:T(8,128)(2,1)S(1)} %shard_map.100) | data formatting | bytes 1048576
Async XLA Ops:
  1.4 2.2 %copy-start = (bf16[1,4096,512]{2,1,0:T(8,128)(2,1)S(1)}, bf16[1,4096,512]{2,1,0:T(8,128)(2,1)}, u32[]{:S(2)}) copy-start(bf16[1,4096,512]{2,1,0:T(8,128)(2,1)} %wq_ref.1) | copy-start | bytes 12582916
  3.6 1.0 %copy-start.1 = (bf16[1,64,4096]{2,1,0:T(8,128)(2,1)S(1)}, bf16[1,64,4096]{2,1,0:T(8,128)(2,1)}, u32[]{:S(2)}) copy-start(bf16[1,64,4096]{2,1,0:T(8,128)(2,1)} %text_ref.1) | copy-start | bytes 1572868
  4.6 0.9 %copy-start.2 = (bf16[2,16,4096]{2,1,0:T(8,128)(2,1)S(1)}, bf16[2,16,4096]{2,1,0:T(8,128)(2,1)}, u32[]{:S(2)}) copy-start(bf16[2,16,4096]{2,1,0:T(8,128)(2,1)} %image_ref.1) | copy-start | bytes 786436
  5.6 0.8 %copy-start.3 = (bf16[1,256,128]{2,1,0:T(8,128)(2,1)S(1)}, bf16[1,256,128]{2,1,0:T(8,128)(2,1)}, u32[]{:S(2)}) copy-start(bf16[1,256,128]{2,1,0:T(8,128)(2,1)} %wk_ref.1) | copy-start | bytes 196612
  6.4 0.8 %copy-start.4 = (bf16[1,256,128]{2,1,0:T(8,128)(2,1)S(1)}, bf16[1,256,128]{2,1,0:T(8,128)(2,1)}, u32[]{:S(2)}) copy-start(bf16[1,256,128]{2,1,0:T(8,128)(2,1)} %wv_ref.1) | copy-start | bytes 196612
  7.3 0.7 %copy-start.5 = (f32[1,128]{1,0:T(1,128)S(1)}, f32[1,128]{1,0:T(1,128)}, u32[]{:S(2)}) copy-start(f32[1,128]{1,0:T(1,128)} %qg_ref.1) | copy-start | bytes 1540
  7.9 0.7 %copy-start.6 = (f32[1,128]{1,0:T(1,128)S(1)}, f32[1,128]{1,0:T(1,128)}, u32[]{:S(2)}) copy-start(f32[1,128]{1,0:T(1,128)} %kg_ref.1) | copy-start | bytes 1540

commit v2 on v1

--- a/solution.py
+++ b/solution.py
@@ -116,6 +116,8 @@
     part_in,
     query_v,
     small,
+    query_gain,
+    key_gain,
     load_sem,
     w_send,
     w_recv,
@@ -162,6 +164,8 @@
         pltpu.make_async_copy(text_ref.at[0], text_v, load_sem.at[3]),
         pltpu.make_async_copy(wq_ref.at[0], wq_v.at[0], load_sem.at[4]),
         pltpu.make_async_copy(wo_ref.at[0], wo_v.at[0], load_sem.at[5]),
+        pltpu.make_async_copy(qg_ref, query_gain, load_sem.at[6]),
+        pltpu.make_async_copy(kg_ref, key_gain, load_sem.at[7]),
     ]
     for load in loads:
         load.start()
@@ -243,8 +247,10 @@
         rows = rows_of((spot + QUAD - distance) % QUAD)
         return across(wkv.at[0, rows], wkv.at[1, rows], relay_send.at[distance], relay_recv.at[distance])
 
-    small[0, 0:1] = qg_ref[...]
-    small[0, 1:2] = kg_ref[...]
+    loads[6].wait()
+    loads[7].wait()
+    small[0, 0:1] = query_gain[...]
+    small[0, 1:2] = key_gain[...]
     small[0, 2:3] = jnp.full((1, head), gate_ref[0], jnp.float32)
 
     loads[0].wait()
@@ -323,7 +329,7 @@
             partial_copy(1, distance).start()
 
     positions = lax.broadcasted_iota(jnp.int32, (tokens, chunk), 0)
-    seen = (positions >= start_ref[core, 0]).astype(jnp.float32)
+    seen = (positions >= start_ref[core]).astype(jnp.float32)
     root_size = math.sqrt(head)
 
     def attend(source, slot, ready):
@@ -410,14 +416,14 @@
     heads = columns // head
     span = QUAD * depth
     groups = 2 * image_rows
-    anywhere = pl.BlockSpec(memory_space=pl.ANY)
+    hbm = pl.BlockSpec(memory_space=pltpu.HBM)
     vmem = pl.BlockSpec(memory_space=pltpu.VMEM)
     smem = pl.BlockSpec(memory_space=pltpu.SMEM)
     dma = pltpu.SemaphoreType.DMA
     return pl.pallas_call(
         functools.partial(kernel, lines),
         out_shape=jax.ShapeDtypeStruct((1, tokens, width), jnp.bfloat16),
-        in_specs=[anywhere, anywhere, smem, anywhere, anywhere, anywhere, anywhere, vmem, vmem, smem],
+        in_specs=[hbm, hbm, smem, hbm, hbm, hbm, hbm, hbm, hbm, smem],
         out_specs=vmem,
         scratch_shapes=[
             pltpu.VMEM((tokens, width), jnp.bfloat16),
@@ -430,7 +436,9 @@
             pltpu.VMEM((lines, 2, groups, 2 * head), jnp.bfloat16),
             pltpu.VMEM((heads * tokens, head), jnp.bfloat16),
             pltpu.VMEM((2, 8, head), jnp.float32),
-            dma((6,)),
+            pltpu.VMEM((1, head), jnp.float32),
+            pltpu.VMEM((1, head), jnp.float32),
+            dma((8,)),
             dma((QUAD, 2)),
             dma((QUAD, 2)),
             dma((lines, 2)),
@@ -445,12 +453,12 @@
             dma((2, lines)),
         ],
         compiler_params=pltpu.CompilerParams(
-            collective_id=0, has_side_effects=True, vmem_limit_bytes=48 * 2**20
+            collective_id=0, has_side_effects=True, vmem_limit_bytes=60 * 2**20
         ),
     )(
         text_states,
         image_states,
-        image_start,
+        image_start.reshape(-1),
         w_query,
         w_key,
         w_value,

time: 33.8 us -> 27.6 us (0.82)
  local copies, waits for them, and re-layouts: 8.7 us -> 1.87 us
  Pallas kernels: 24.1 us -> 24.9 us
    unnamed x16 -> x1, local copies, waits for them, and re-layouts: 8.7 us -> 1.87 us
    pallas_call x1, Pallas kernels: 24.1 us -> 24.9 us  [local_fused(): pl.pallas_call(functools.partial(kernel, lines), out_shape=jax.ShapeDtype...]
where the time goes in v2:
time: 27.6 us; the launch traced here: 27.4 us
  Pallas kernels  24.9 us (90%)
  local copies, waits for them, and re-layouts  1.87 us (7%)
  between operations  0.66 us (2%)
    pallas_call x1, Pallas kernels, local_fused(): pl.pallas_call(functools.partial(kernel, lines), out_shape=jax.ShapeDtype...  24.9 us
    unnamed x1, local copies, waits for them, and re-layouts  1.87 us

profile of v2, /device:TPU:0, one launch (start us, length us, event | category | flops | bytes accessed | tf_op | source)
XLA Modules:
  0.0 27.4 jit_solution(13249805607070912897)
XLA Ops:
  0.7 24.9 %shard_map.100 = bf16[1,64,4096]{2,1,0:T(8,128)(2,1)} custom-call(bf16[1,64,4096]{2,1,0:T(8,128)(2,1)} %text_ref.1, bf16[2,16,4096]{2,1,0:T(8,128)(2,1)} %image_ref.1, s32[2]{0:T(128)} %bitcast.1, bf16[1,4096,512]{2,1,0:T(8,128)(2,1)} %wq_ref.1, bf16[1,256,128]{2,1,0:T(8,128)(2,1)} %wk_ref.1, bf16[1,256,128]{2,1,0:T(8,128)(2,1)} %wv_ref.1, ...), custom_call_target="tpu_custom_call" | custom-call | tf_op jit(solution)/shard_map/pallas_call | solution.py:423
  25.5 1.9 %copy.13 = bf16[1,64,4096]{2,1,0:T(8,128)(2,1)} copy(bf16[1,64,4096]{2,1,0:T(8,128)(2,1)} %shard_map.100) | data formatting | bytes 1048576

commit v3 on v2

--- a/solution.py
+++ b/solution.py
@@ -109,6 +109,9 @@
     text_v,
     wq_v,
     wo_v,
+    joint_sum,
+    joint,
+    first,
     wkv,
     img,
     part,
@@ -118,6 +121,7 @@
     small,
     query_gain,
     key_gain,
+    starts,
     load_sem,
     w_send,
     w_recv,
@@ -127,8 +131,8 @@
     relay_recv,
     big_send,
     big_recv,
-    small_send,
-    small_recv,
+    one_send,
+    one_recv,
     p_send,
     p_recv,
 ):
@@ -139,7 +143,7 @@
     spot = place % QUAD
     depth = wk_ref.shape[1]
     head = wk_ref.shape[2]
-    tokens, width = text_v.shape
+    tokens, width = text_v.shape[1:]
     heads = wq_ref.shape[2] // head
     image_rows = image_ref.shape[1]
     span = QUAD * depth
@@ -161,11 +165,12 @@
             img.at[line, pl.ds(pl.multiple_of(core * image_rows, image_rows), image_rows)],
             load_sem.at[2],
         ),
-        pltpu.make_async_copy(text_ref.at[0], text_v, load_sem.at[3]),
-        pltpu.make_async_copy(wq_ref.at[0], wq_v.at[0], load_sem.at[4]),
+        pltpu.make_async_copy(text_ref.at[0], text_v.at[0], load_sem.at[3]),
+        pltpu.make_async_copy(wq_ref.at[0], wq_v, load_sem.at[4]),
         pltpu.make_async_copy(wo_ref.at[0], wo_v.at[0], load_sem.at[5]),
         pltpu.make_async_copy(qg_ref, query_gain, load_sem.at[6]),
         pltpu.make_async_copy(kg_ref, key_gain, load_sem.at[7]),
+        pltpu.make_async_copy(start_ref, starts, load_sem.at[8]),
     ]
     for load in loads:
         load.start()
@@ -221,27 +226,20 @@
             device_id_type=MESH,
         )
 
-    query_rows = width // PIECES
-    out_rows = wo_ref.shape[1] // PIECES
-    query_pieces = [
+    stretch = width // PIECES
+    out_pieces = [
         across(
-            wq_ref.at[0, pl.ds(i * query_rows, query_rows)],
-            wq_v.at[1, pl.ds(i * query_rows, query_rows)],
-            big_send.at[0, i],
-            big_recv.at[0, i],
+            wo_ref.at[0, :, pl.ds(i * stretch, stretch)],
+            wo_v.at[1, :, pl.ds(i * stretch, stretch)],
+            big_send.at[i],
+            big_recv.at[i],
         )
         for i in range(PIECES)
     ]
-    out_pieces = [
-        across(
-            wo_ref.at[0, pl.ds(i * out_rows, out_rows)],
-            wo_v.at[1, pl.ds(i * out_rows, out_rows)],
-            big_send.at[1, i],
-            big_recv.at[1, i],
-        )
-        for i in range(PIECES)
-    ]
-    small_copy = across(small.at[0], small.at[1], small_send, small_recv)
+    small_copy = across(small.at[0], small.at[1], one_send.at[0], one_recv.at[0])
+    text_copy = across(text_ref.at[0], text_v.at[1], one_send.at[1], one_recv.at[1])
+    first_copy = across(first.at[0], first.at[1], one_send.at[2], one_recv.at[2])
+    joint_copy = across(joint.at[0], joint.at[1], one_send.at[3], one_recv.at[3])
 
     def relay(distance):
         rows = rows_of((spot + QUAD - distance) % QUAD)
@@ -256,37 +254,57 @@
     loads[0].wait()
     loads[1].wait()
 
+    @pl.when(core == 0)
+    def _():
+        text_copy.start()
+        for piece in out_pieces:
+            piece.start()
+
     @pl.when(core == 1)
     def _():
         small_copy.start()
         relay(0).start()
-        for piece in query_pieces:
+        for piece in out_pieces[: PIECES // 2]:
             piece.start()
+
+    chunk = 512
+
+    def project(slot):
+        def step(i, total):
+            at = pl.ds(pl.multiple_of(i * chunk, chunk), chunk)
+            return total + jnp.dot(text_v[slot, :, at], wq_v[at, :], preferred_element_type=jnp.float32)
+
+        return lax.fori_loop(0, width // chunk, step, jnp.zeros((tokens, heads * head), jnp.float32))
+
+    def store_queries(sums, slot):
+        for h in range(heads):
+            query_v[h * tokens : (h + 1) * tokens, :] = normalized(
+                sums[:, h * head : (h + 1) * head], small[slot, 0:1]
+            ).astype(jnp.bfloat16)
+
+    def join(i):
+        out_pieces[i].wait_recv()
+        at = pl.ds(i * stretch, stretch)
+        product = jnp.dot(wo_v[1, :, at], wq_v[at, :], preferred_element_type=jnp.float32)
+        joint_sum[...] = product if i == 0 else joint_sum[...] + product
+
+    loads[3].wait()
+    loads[4].wait()
+    store_queries(project(0), 0)
+
+    @pl.when(core == 1)
+    def _():
         for distance in range(1, QUAD):
             weight_copies[2 * distance - 2].wait_recv()
             weight_copies[2 * distance - 1].wait_recv()
             relay(distance).start()
-        for piece in out_pieces:
+        for piece in out_pieces[PIECES // 2 :]:
             piece.start()
-
-    chunk = 512
-
-    def project(source, slot):
-        steps = width // chunk
-
-        def step(i, total):
-            at = pl.ds(pl.multiple_of(i * chunk, chunk), chunk)
-            return total + jnp.dot(source[:, at], wq_v[slot, at, :], preferred_element_type=jnp.float32)
-
-        sums = lax.fori_loop(0, steps, step, jnp.zeros((tokens, heads * head), jnp.float32))
-        for h in range(heads):
-            query_v[h * tokens : (h + 1) * tokens, :] = normalized(
-                sums[:, h * head : (h + 1) * head], small[slot, 0:1]
-            ).astype(jnp.bfloat16)
-
-    loads[3].wait()
-    loads[4].wait()
-    project(text_v, 0)
+        text_copy.wait_recv()
+        first[0] = project(1)
+        first_copy.start()
+        for i in range(PIECES // 2):
+            join(i)
 
     loads[2].wait()
     for copy in image_copies:
@@ -320,6 +338,13 @@
     for distance in range(1, lines):
         partial_copy(0, distance).start()
 
+    @pl.when(core == 1)
+    def _():
+        for i in range(PIECES // 2, PIECES):
+            join(i)
+        joint[0] = joint_sum[...].astype(jnp.bfloat16)
+        joint_copy.start()
+
     @pl.when(core == 0)
     def _():
         for distance in range(QUAD):
@@ -328,11 +353,12 @@
         for distance in range(1, lines):
             partial_copy(1, distance).start()
 
-    positions = lax.broadcasted_iota(jnp.int32, (tokens, chunk), 0)
-    seen = (positions >= start_ref[core]).astype(jnp.float32)
+    positions = lax.broadcasted_iota(jnp.int32, (tokens, 1), 0)
+    loads[8].wait()
+    seen = (positions >= starts[core]).astype(jnp.float32)
     root_size = math.sqrt(head)
 
-    def attend(source, slot, ready):
+    def attend(slot):
         total = part[line, slot]
         for distance in range(1, lines):
             partial_copy(slot, distance).wait_recv()
@@ -351,49 +377,53 @@
         attended = jnp.concatenate(
             [attended[h * tokens : (h + 1) * tokens] for h in range(heads)], axis=1
         )
-        factor = jnp.tanh(small[slot, 2:3])[:, 0:1] * seen
-        ready()
-
+        return attended, jnp.tanh(small[slot, 2:3])[:, 0:1] * seen
+
+    def advance(source, slot, attended, factor):
         def step(i, carry):
             at = pl.ds(pl.multiple_of(i * chunk, chunk), chunk)
             update = jnp.dot(attended, wo_v[slot, :, at], preferred_element_type=jnp.float32)
-            out_ref[0, :, at] = (source(at).astype(jnp.float32) + factor * update).astype(jnp.bfloat16)
+            out_ref[0, :, at] = (source[:, at].astype(jnp.float32) + factor * update).astype(jnp.bfloat16)
             return carry
 
         lax.fori_loop(0, width // chunk, step, 0)
 
-    attend(lambda at: text_v[:, at], 0, loads[5].wait)
+    attended, factor = attend(0)
+    loads[5].wait()
+    advance(text_v.at[0], 0, attended, factor)
 
     @pl.when(core == 0)
     def _():
         small_copy.wait_recv()
-        for piece in query_pieces:
+        first_copy.wait_recv()
+        joint_copy.wait_recv()
+        change = jnp.dot(attended, joint[1], preferred_element_type=jnp.float32)
+        store_queries(first[1] + factor * change, 1)
+        later, later_factor = attend(1)
+        for piece in out_pieces:
             piece.wait_recv()
-        project(out_ref.at[0], 1)
-
-        def ready():
-            for piece in out_pieces:
-                piece.wait_recv()
-
-        attend(lambda at: out_ref[0, :, at], 1, ready)
+        advance(out_ref.at[0], 1, later, later_factor)
 
     for copy in image_copies + weight_copies:
         copy.wait_send()
     for distance in range(1, lines):
         partial_copy(0, distance).wait_send()
 
+    for piece in out_pieces:
+        piece.wait_send()
+
     @pl.when(core == 0)
     def _():
         for distance in range(1, lines):
             partial_copy(1, distance).wait_send()
+        text_copy.wait_send()
 
     @pl.when(core == 1)
     def _():
-        small_copy.wait_send()
         for distance in range(QUAD):
             relay(distance).wait_send()
-        for piece in query_pieces + out_pieces:
-            piece.wait_send()
+        for copy in (small_copy, first_copy, joint_copy):
+            copy.wait_send()
 
 
 def local_fused(
@@ -423,12 +453,15 @@
     return pl.pallas_call(
         functools.partial(kernel, lines),
         out_shape=jax.ShapeDtypeStruct((1, tokens, width), jnp.bfloat16),
-        in_specs=[hbm, hbm, smem, hbm, hbm, hbm, hbm, hbm, hbm, smem],
+        in_specs=[hbm, hbm, hbm, hbm, hbm, hbm, hbm, hbm, hbm, smem],
         out_specs=vmem,
         scratch_shapes=[
-            pltpu.VMEM((tokens, width), jnp.bfloat16),
-            pltpu.VMEM((2, width, columns), jnp.bfloat16),
+            pltpu.VMEM((2, tokens, width), jnp.bfloat16),
+            pltpu.VMEM((width, columns), jnp.bfloat16),
             pltpu.VMEM((2, columns, width), jnp.bfloat16),
+            pltpu.VMEM((columns, columns), jnp.float32),
+            pltpu.VMEM((2, columns, columns), jnp.bfloat16),
+            pltpu.VMEM((2, tokens, columns), jnp.float32),
             pltpu.VMEM((2, span, 2 * head), jnp.bfloat16),
             pltpu.VMEM((lines, groups, span), jnp.bfloat16),
             pltpu.VMEM((lines, 2, groups, 2 * head), jnp.float32),
@@ -438,33 +471,34 @@
             pltpu.VMEM((2, 8, head), jnp.float32),
             pltpu.VMEM((1, head), jnp.float32),
             pltpu.VMEM((1, head), jnp.float32),
-            dma((8,)),
+            pltpu.SMEM(image_start.shape[:1], jnp.int32),
+            dma((9,)),
             dma((QUAD, 2)),
             dma((QUAD, 2)),
             dma((lines, 2)),
             dma((lines, 2)),
             dma((QUAD,)),
             dma((QUAD,)),
-            dma((2, PIECES)),
-            dma((2, PIECES)),
-            dma,
-            dma,
+            dma((PIECES,)),
+            dma((PIECES,)),
+            dma((4,)),
+            dma((4,)),
             dma((2, lines)),
             dma((2, lines)),
         ],
         compiler_params=pltpu.CompilerParams(
-            collective_id=0, has_side_effects=True, vmem_limit_bytes=60 * 2**20
+            collective_id=0, has_side_effects=True, vmem_limit_bytes=48 * 2**20
         ),
     )(
-        text_states,
-        image_states,
-        image_start.reshape(-1),
-        w_query,
-        w_key,
-        w_value,
-        w_out,
-        query_gain,
-        key_gain,
+        pltpu.with_memory_space_constraint(text_states, pltpu.HBM),
+        pltpu.with_memory_space_constraint(image_states, pltpu.HBM),
+        pltpu.with_memory_space_constraint(image_start.reshape(-1), pltpu.HBM),
+        pltpu.with_memory_space_constraint(w_query, pltpu.HBM),
+        pltpu.with_memory_space_constraint(w_key, pltpu.HBM),
+        pltpu.with_memory_space_constraint(w_value, pltpu.HBM),
+        pltpu.with_memory_space_constraint(w_out, pltpu.HBM),
+        pltpu.with_memory_space_constraint(query_gain, pltpu.HBM),
+        pltpu.with_memory_space_constraint(key_gain, pltpu.HBM),
         cross_gate,
     )
 

time: 27.6 us -> 23.9 us (0.87)
  Pallas kernels: 24.9 us -> 22.3 us
  local copies, waits for them, and re-layouts: 1.87 us -> 0.8 us
    pallas_call x1, Pallas kernels: 24.9 us -> 22.3 us  [local_fused(): pl.pallas_call(functools.partial(kernel, lines), out_shape=jax.ShapeDtype...]
    unnamed x1, local copies, waits for them, and re-layouts: 1.87 us -> 0.8 us
where the time goes in v3:
time: 23.9 us; the launch traced here: 23.8 us
  Pallas kernels  22.3 us (93%)
  local copies, waits for them, and re-layouts  0.8 us (3%)
  between operations  0.66 us (3%)
    pallas_call x1, Pallas kernels, local_fused(): pl.pallas_call(functools.partial(kernel, lines), out_shape=jax.ShapeDtype...  22.3 us
    unnamed x1, local copies, waits for them, and re-layouts  0.8 us

profile of v3, /device:TPU:0, one launch (start us, length us, event | category | flops | bytes accessed | tf_op | source)
XLA Modules:
  0.0 23.8 jit_solution(9499089250982264224)
XLA Ops:
  0.7 22.3 %shard_map.100 = bf16[1,64,4096]{2,1,0:T(8,128)(2,1)S(1)} custom-call(bf16[1,64,4096]{2,1,0:T(8,128)(2,1)} %text_ref.1, bf16[2,16,4096]{2,1,0:T(8,128)(2,1)} %image_ref.1, s32[2]{0:T(128)} %bitcast.1, bf16[1,4096,512]{2,1,0:T(8,128)(2,1)} %wq_ref.1, bf16[1,256,128]{2,1,0:T(8,128)(2,1)} %wk_ref.1, bf16[1,256,128]{2,1,0:T(8,128)(2,1)} %wv_ref.1, ...), custom_call_target="tpu_custom_call" | custom-call | tf_op jit(solution)/shard_map/pallas_call | solution.py:453
  23.0 0.8 %copy.13 = bf16[1,64,4096]{2,1,0:T(8,128)(2,1)} copy(bf16[1,64,4096]{2,1,0:T(8,128)(2,1)S(1)} %shard_map.100) | data formatting | bytes 1048576

commit v4 on v3

--- a/solution.py
+++ b/solution.py
@@ -108,6 +108,7 @@
     out_ref,
     text_v,
     wq_v,
+    wq_half,
     wo_v,
     joint_sum,
     joint,
@@ -231,10 +232,20 @@
         across(
             wo_ref.at[0, :, pl.ds(i * stretch, stretch)],
             wo_v.at[1, :, pl.ds(i * stretch, stretch)],
-            big_send.at[i],
-            big_recv.at[i],
+            big_send.at[0, i],
+            big_recv.at[0, i],
         )
         for i in range(PIECES)
+    ]
+    half = PIECES // 2
+    query_pieces = [
+        across(
+            wq_ref.at[0, pl.ds(i * stretch, stretch)],
+            wq_half.at[pl.ds(i * stretch, stretch)],
+            big_send.at[1, i],
+            big_recv.at[1, i],
+        )
+        for i in range(half)
     ]
     small_copy = across(small.at[0], small.at[1], one_send.at[0], one_recv.at[0])
     text_copy = across(text_ref.at[0], text_v.at[1], one_send.at[1], one_recv.at[1])
@@ -257,24 +268,28 @@
     @pl.when(core == 0)
     def _():
         text_copy.start()
-        for piece in out_pieces:
+        for piece in out_pieces[half:]:
             piece.start()
 
     @pl.when(core == 1)
     def _():
         small_copy.start()
         relay(0).start()
-        for piece in out_pieces[: PIECES // 2]:
+        for piece in query_pieces:
             piece.start()
 
     chunk = 512
 
-    def project(slot):
+    def project(slots):
+        rows = slots * tokens
+
         def step(i, total):
             at = pl.ds(pl.multiple_of(i * chunk, chunk), chunk)
-            return total + jnp.dot(text_v[slot, :, at], wq_v[at, :], preferred_element_type=jnp.float32)
-
-        return lax.fori_loop(0, width // chunk, step, jnp.zeros((tokens, heads * head), jnp.float32))
+            return total + jnp.dot(
+                text_v[:slots, :, at].reshape(rows, chunk), wq_v[at, :], preferred_element_type=jnp.float32
+            )
+
+        return lax.fori_loop(0, width // chunk, step, jnp.zeros((rows, heads * head), jnp.float32))
 
     def store_queries(sums, slot):
         for h in range(heads):
@@ -282,29 +297,44 @@
                 sums[:, h * head : (h + 1) * head], small[slot, 0:1]
             ).astype(jnp.bfloat16)
 
-    def join(i):
-        out_pieces[i].wait_recv()
-        at = pl.ds(i * stretch, stretch)
-        product = jnp.dot(wo_v[1, :, at], wq_v[at, :], preferred_element_type=jnp.float32)
+    def join(i, left, right):
+        product = jnp.dot(left, right, preferred_element_type=jnp.float32)
         joint_sum[...] = product if i == 0 else joint_sum[...] + product
 
     loads[3].wait()
     loads[4].wait()
-    store_queries(project(0), 0)
+
+    @pl.when(core == 0)
+    def _():
+        store_queries(project(1), 0)
+        loads[5].wait()
+        for i in range(half):
+            query_pieces[i].wait_recv()
+            at = pl.ds(i * stretch, stretch)
+            join(i, wo_v[0, :, at], wq_half[at, :])
 
     @pl.when(core == 1)
     def _():
+        text_copy.wait_recv()
+        sums = project(2)
+        store_queries(sums[:tokens], 0)
+        first[0] = sums[tokens:]
+        first_copy.start()
+        for piece in out_pieces[:half]:
+            piece.start()
+        for i in range(half):
+            out_pieces[half + i].wait_recv()
+            at = pl.ds((half + i) * stretch, stretch)
+            join(i, wo_v[1, :, at], wq_v[at, :])
+        joint[0] = joint_sum[...].astype(jnp.bfloat16)
+        joint_copy.start()
         for distance in range(1, QUAD):
             weight_copies[2 * distance - 2].wait_recv()
             weight_copies[2 * distance - 1].wait_recv()
             relay(distance).start()
-        for piece in out_pieces[PIECES // 2 :]:
+        for piece in out_pieces[half:]:
             piece.start()
-        text_copy.wait_recv()
-        first[0] = project(1)
-        first_copy.start()
-        for i in range(PIECES // 2):
-            join(i)
+        loads[5].wait()
 
     loads[2].wait()
     for copy in image_copies:
@@ -338,13 +368,6 @@
     for distance in range(1, lines):
         partial_copy(0, distance).start()
 
-    @pl.when(core == 1)
-    def _():
-        for i in range(PIECES // 2, PIECES):
-            join(i)
-        joint[0] = joint_sum[...].astype(jnp.bfloat16)
-        joint_copy.start()
-
     @pl.when(core == 0)
     def _():
         for distance in range(QUAD):
@@ -352,6 +375,10 @@
         partial_sums(1)
         for distance in range(1, lines):
             partial_copy(1, distance).start()
+        small_copy.wait_recv()
+        first_copy.wait_recv()
+        joint_copy.wait_recv()
+        joint[0] = (joint_sum[...] + joint[1].astype(jnp.float32)).astype(jnp.bfloat16)
 
     positions = lax.broadcasted_iota(jnp.int32, (tokens, 1), 0)
     loads[8].wait()
@@ -389,27 +416,27 @@
         lax.fori_loop(0, width // chunk, step, 0)
 
     attended, factor = attend(0)
-    loads[5].wait()
-    advance(text_v.at[0], 0, attended, factor)
 
     @pl.when(core == 0)
     def _():
-        small_copy.wait_recv()
-        first_copy.wait_recv()
-        joint_copy.wait_recv()
-        change = jnp.dot(attended, joint[1], preferred_element_type=jnp.float32)
+        change = jnp.dot(attended, joint[0], preferred_element_type=jnp.float32)
         store_queries(first[1] + factor * change, 1)
         later, later_factor = attend(1)
+        advance(text_v.at[0], 0, attended, factor)
         for piece in out_pieces:
             piece.wait_recv()
         advance(out_ref.at[0], 1, later, later_factor)
+
+    @pl.when(core == 1)
+    def _():
+        advance(text_v.at[0], 0, attended, factor)
 
     for copy in image_copies + weight_copies:
         copy.wait_send()
     for distance in range(1, lines):
         partial_copy(0, distance).wait_send()
 
-    for piece in out_pieces:
+    for piece in out_pieces[half:]:
         piece.wait_send()
 
     @pl.when(core == 0)
@@ -422,7 +449,7 @@
     def _():
         for distance in range(QUAD):
             relay(distance).wait_send()
-        for copy in (small_copy, first_copy, joint_copy):
+        for copy in [small_copy, first_copy, joint_copy] + query_pieces + out_pieces[:half]:
             copy.wait_send()
 
 
@@ -458,6 +485,7 @@
         scratch_shapes=[
             pltpu.VMEM((2, tokens, width), jnp.bfloat16),
             pltpu.VMEM((width, columns), jnp.bfloat16),
+            pltpu.VMEM((width // 2, columns), jnp.bfloat16),
             pltpu.VMEM((2, columns, width), jnp.bfloat16),
             pltpu.VMEM((columns, columns), jnp.float32),
             pltpu.VMEM((2, columns, columns), jnp.bfloat16),
@@ -479,8 +507,8 @@
             dma((lines, 2)),
             dma((QUAD,)),
             dma((QUAD,)),
-            dma((PIECES,)),
-            dma((PIECES,)),
+            dma((2, PIECES)),
+            dma((2, PIECES)),
             dma((4,)),
             dma((4,)),
             dma((2, lines)),

time: 23.9 us -> 25.9 us (1.084)
  Pallas kernels: 22.3 us -> 24.3 us
    pallas_call x1, Pallas kernels: 22.3 us -> 24.3 us  [local_fused(): pl.pallas_call(functools.partial(kernel, lines), out_shape=jax.ShapeDtype...]
where the time goes in v4:
time: 25.9 us; the launch traced here: 25.8 us
  Pallas kernels  24.3 us (94%)
  local copies, waits for them, and re-layouts  0.8 us (3%)
  between operations  0.66 us (3%)
    pallas_call x1, Pallas kernels, local_fused(): pl.pallas_call(functools.partial(kernel, lines), out_shape=jax.ShapeDtype...  24.3 us
    unnamed x1, local copies, waits for them, and re-layouts  0.8 us

profile of v4, /device:TPU:0, one launch (start us, length us, event | category | flops | bytes accessed | tf_op | source)
XLA Modules:
  0.0 25.8 jit_solution(10958270667996066754)
XLA Ops:
  0.7 24.3 %shard_map.100 = bf16[1,64,4096]{2,1,0:T(8,128)(2,1)S(1)} custom-call(bf16[1,64,4096]{2,1,0:T(8,128)(2,1)} %text_ref.1, bf16[2,16,4096]{2,1,0:T(8,128)(2,1)} %image_ref.1, s32[2]{0:T(128)} %bitcast.1, bf16[1,4096,512]{2,1,0:T(8,128)(2,1)} %wq_ref.1, bf16[1,256,128]{2,1,0:T(8,128)(2,1)} %wk_ref.1, bf16[1,256,128]{2,1,0:T(8,128)(2,1)} %wv_ref.1, ...), custom_call_target="tpu_custom_call" | custom-call | tf_op jit(solution)/shard_map/pallas_call | solution.py:480
  25.0 0.8 %copy.13 = bf16[1,64,4096]{2,1,0:T(8,128)(2,1)} copy(bf16[1,64,4096]{2,1,0:T(8,128)(2,1)S(1)} %shard_map.100) | data formatting | bytes 1048576

commit v5 on v4

--- a/solution.py
+++ b/solution.py
@@ -113,6 +113,8 @@
     joint_sum,
     joint,
     first,
+    mixed,
+    back,
     wkv,
     img,
     part,
@@ -134,6 +136,8 @@
     big_recv,
     one_send,
     one_recv,
+    back_send,
+    back_recv,
     p_send,
     p_recv,
 ):
@@ -251,6 +255,17 @@
     text_copy = across(text_ref.at[0], text_v.at[1], one_send.at[1], one_recv.at[1])
     first_copy = across(first.at[0], first.at[1], one_send.at[2], one_recv.at[2])
     joint_copy = across(joint.at[0], joint.at[1], one_send.at[3], one_recv.at[3])
+    mixed_copies = [across(mixed.at[i], mixed.at[2 + i], one_send.at[4 + i], one_recv.at[4 + i]) for i in range(2)]
+    quarter = stretch // 2
+    back_copies = [
+        across(
+            back.at[:, pl.ds(i * quarter, quarter)],
+            out_ref.at[0, :, pl.ds((PIECES + i) * quarter, quarter)],
+            back_send.at[i],
+            back_recv.at[i],
+        )
+        for i in range(PIECES)
+    ]
 
     def relay(distance):
         rows = rows_of((spot + QUAD - distance) % QUAD)
@@ -265,6 +280,8 @@
     loads[0].wait()
     loads[1].wait()
 
+    small_copy.start()
+
     @pl.when(core == 0)
     def _():
         text_copy.start()
@@ -273,7 +290,6 @@
 
     @pl.when(core == 1)
     def _():
-        small_copy.start()
         relay(0).start()
         for piece in query_pieces:
             piece.start()
@@ -303,42 +319,6 @@
 
     loads[3].wait()
     loads[4].wait()
-
-    @pl.when(core == 0)
-    def _():
-        store_queries(project(1), 0)
-        loads[5].wait()
-        for i in range(half):
-            query_pieces[i].wait_recv()
-            at = pl.ds(i * stretch, stretch)
-            join(i, wo_v[0, :, at], wq_half[at, :])
-
-    @pl.when(core == 1)
-    def _():
-        text_copy.wait_recv()
-        sums = project(2)
-        store_queries(sums[:tokens], 0)
-        first[0] = sums[tokens:]
-        first_copy.start()
-        for piece in out_pieces[:half]:
-            piece.start()
-        for i in range(half):
-            out_pieces[half + i].wait_recv()
-            at = pl.ds((half + i) * stretch, stretch)
-            join(i, wo_v[1, :, at], wq_v[at, :])
-        joint[0] = joint_sum[...].astype(jnp.bfloat16)
-        joint_copy.start()
-        for distance in range(1, QUAD):
-            weight_copies[2 * distance - 2].wait_recv()
-            weight_copies[2 * distance - 1].wait_recv()
-            relay(distance).start()
-        for piece in out_pieces[half:]:
-            piece.start()
-        loads[5].wait()
-
-    loads[2].wait()
-    for copy in image_copies:
-        copy.wait_recv()
 
     def partial_sums(slot):
         groups = 2 * image_rows
@@ -359,30 +339,72 @@
             device_id_type=MESH,
         )
 
+    def arrived():
+        loads[2].wait()
+        for copy in image_copies:
+            copy.wait_recv()
+
+    def return_partials(slot):
+        partial_sums(slot)
+        for distance in range(1, lines):
+            partial_copy(slot, distance).start()
+
     @pl.when(core == 0)
     def _():
+        def join_own(i):
+            query_pieces[i].wait_recv()
+            at = pl.ds(i * stretch, stretch)
+            join(i, wo_v[0, :, at], wq_half[at, :])
+
+        store_queries(project(1), 0)
+        loads[5].wait()
+        for i in range(half - 1):
+            join_own(i)
         for copy in weight_copies:
             copy.wait_recv()
-
-    partial_sums(0)
-    for distance in range(1, lines):
-        partial_copy(0, distance).start()
-
-    @pl.when(core == 0)
-    def _():
+        arrived()
+        return_partials(0)
         for distance in range(QUAD):
             relay(distance).wait_recv()
-        partial_sums(1)
-        for distance in range(1, lines):
-            partial_copy(1, distance).start()
+        return_partials(1)
+        join_own(half - 1)
         small_copy.wait_recv()
         first_copy.wait_recv()
         joint_copy.wait_recv()
         joint[0] = (joint_sum[...] + joint[1].astype(jnp.float32)).astype(jnp.bfloat16)
 
+    @pl.when(core == 1)
+    def _():
+        def join_own(i):
+            out_pieces[half + i].wait_recv()
+            at = pl.ds((half + i) * stretch, stretch)
+            join(i, wo_v[1, :, at], wq_v[at, :])
+
+        text_copy.wait_recv()
+        sums = project(2)
+        store_queries(sums[:tokens], 0)
+        first[0] = sums[tokens:]
+        first_copy.start()
+        for i in range(half - 1):
+            join_own(i)
+        for distance in range(1, QUAD):
+            weight_copies[2 * distance - 2].wait_recv()
+            weight_copies[2 * distance - 1].wait_recv()
+            relay(distance).start()
+        for piece in out_pieces[:half]:
+            piece.start()
+        arrived()
+        return_partials(0)
+        join_own(half - 1)
+        joint[0] = joint_sum[...].astype(jnp.bfloat16)
+        joint_copy.start()
+        loads[5].wait()
+        small_copy.wait_recv()
+
     positions = lax.broadcasted_iota(jnp.int32, (tokens, 1), 0)
     loads[8].wait()
     seen = (positions >= starts[core]).astype(jnp.float32)
+    seen_other = (positions >= starts[other]).astype(jnp.float32)
     root_size = math.sqrt(head)
 
     def attend(slot):
@@ -404,52 +426,80 @@
         attended = jnp.concatenate(
             [attended[h * tokens : (h + 1) * tokens] for h in range(heads)], axis=1
         )
-        return attended, jnp.tanh(small[slot, 2:3])[:, 0:1] * seen
+        return attended
+
+    def gate(slot):
+        return jnp.tanh(small[slot, 2:3])[:, 0:1]
+
+    def update(values, slot, at):
+        return jnp.dot(values, wo_v[slot, :, at], preferred_element_type=jnp.float32)
 
     def advance(source, slot, attended, factor):
-        def step(i, carry):
-            at = pl.ds(pl.multiple_of(i * chunk, chunk), chunk)
-            update = jnp.dot(attended, wo_v[slot, :, at], preferred_element_type=jnp.float32)
-            out_ref[0, :, at] = (source[:, at].astype(jnp.float32) + factor * update).astype(jnp.bfloat16)
-            return carry
-
-        lax.fori_loop(0, width // chunk, step, 0)
-
-    attended, factor = attend(0)
+        for i in range(PIECES):
+            at = pl.ds(i * quarter, quarter)
+            out_ref[0, :, at] = (source[:, at].astype(jnp.float32) + factor * update(attended, slot, at)).astype(
+                jnp.bfloat16
+            )
+
+    attended = attend(0)
+    factor = gate(0) * seen
 
     @pl.when(core == 0)
     def _():
+        mixed[0] = attended
+        mixed_copies[0].start()
         change = jnp.dot(attended, joint[0], preferred_element_type=jnp.float32)
         store_queries(first[1] + factor * change, 1)
-        later, later_factor = attend(1)
+        later = attend(1)
+        mixed[1] = later
+        mixed_copies[1].start()
         advance(text_v.at[0], 0, attended, factor)
-        for piece in out_pieces:
+        for piece in out_pieces[:half]:
             piece.wait_recv()
-        advance(out_ref.at[0], 1, later, later_factor)
+        advance(out_ref.at[0], 1, later, gate(1) * seen)
+        for copy in back_copies:
+            copy.wait_recv()
 
     @pl.when(core == 1)
     def _():
         advance(text_v.at[0], 0, attended, factor)
+        mixed_copies[0].wait_recv()
+        before = gate(1) * seen_other
+        for i in range(PIECES):
+            at = pl.ds((PIECES + i) * quarter, quarter)
+            back[:, i * quarter : (i + 1) * quarter] = (
+                text_v[1, :, at].astype(jnp.float32) + before * update(mixed[2], 1, at)
+            ).astype(jnp.bfloat16)
+        mixed_copies[1].wait_recv()
+        both = jnp.concatenate([attended, mixed[3]], axis=0)
+        after = gate(0) * seen_other
+        for i in range(PIECES):
+            at = pl.ds((PIECES + i) * quarter, quarter)
+            here = pl.ds(i * quarter, quarter)
+            sums = update(both, 0, at)
+            back[:, here] = (back[:, here].astype(jnp.float32) + after * sums[tokens:]).astype(jnp.bfloat16)
+            back_copies[i].start()
+            out_ref[0, :, at] = (text_v[0, :, at].astype(jnp.float32) + factor * sums[:tokens]).astype(jnp.bfloat16)
 
     for copy in image_copies + weight_copies:
         copy.wait_send()
     for distance in range(1, lines):
         partial_copy(0, distance).wait_send()
 
-    for piece in out_pieces[half:]:
-        piece.wait_send()
+    small_copy.wait_send()
 
     @pl.when(core == 0)
     def _():
         for distance in range(1, lines):
             partial_copy(1, distance).wait_send()
-        text_copy.wait_send()
+        for copy in [text_copy] + mixed_copies + out_pieces[half:]:
+            copy.wait_send()
 
     @pl.when(core == 1)
     def _():
         for distance in range(QUAD):
             relay(distance).wait_send()
-        for copy in [small_copy, first_copy, joint_copy] + query_pieces + out_pieces[:half]:
+        for copy in [first_copy, joint_copy] + query_pieces + out_pieces[:half] + back_copies:
             copy.wait_send()
 
 
@@ -490,6 +540,8 @@
             pltpu.VMEM((columns, columns), jnp.float32),
             pltpu.VMEM((2, columns, columns), jnp.bfloat16),
             pltpu.VMEM((2, tokens, columns), jnp.float32),
+            pltpu.VMEM((4, tokens, columns), jnp.bfloat16),
+            pltpu.VMEM((tokens, width // 2), jnp.bfloat16),
             pltpu.VMEM((2, span, 2 * head), jnp.bfloat16),
             pltpu.VMEM((lines, groups, span), jnp.bfloat16),
             pltpu.VMEM((lines, 2, groups, 2 * head), jnp.float32),
@@ -509,8 +561,10 @@
             dma((QUAD,)),
             dma((2, PIECES)),
             dma((2, PIECES)),
-            dma((4,)),
-            dma((4,)),
+            dma((6,)),
+            dma((6,)),
+            dma((PIECES,)),
+            dma((PIECES,)),
             dma((2, lines)),
             dma((2, lines)),
         ],

time: 25.9 us -> 24.1 us (0.931)
  Pallas kernels: 24.3 us -> 22.5 us
    pallas_call x1, Pallas kernels: 24.3 us -> 22.5 us  [local_fused(): pl.pallas_call(functools.partial(kernel, lines), out_shape=jax.ShapeDtype...]
where the time goes in v5:
time: 24.1 us; the launch traced here: 23.9 us
  Pallas kernels  22.5 us (93%)
  local copies, waits for them, and re-layouts  0.8 us (3%)
  between operations  0.66 us (3%)
    pallas_call x1, Pallas kernels, local_fused(): pl.pallas_call(functools.partial(kernel, lines), out_shape=jax.ShapeDtype...  22.5 us
    unnamed x1, local copies, waits for them, and re-layouts  0.8 us

profile of v5, /device:TPU:0, one launch (start us, length us, event | category | flops | bytes accessed | tf_op | source)
XLA Modules:
  0.0 23.9 jit_solution(1313087673137943704)
XLA Ops:
  0.7 22.5 %shard_map.100 = bf16[1,64,4096]{2,1,0:T(8,128)(2,1)S(1)} custom-call(bf16[1,64,4096]{2,1,0:T(8,128)(2,1)} %text_ref.1, bf16[2,16,4096]{2,1,0:T(8,128)(2,1)} %image_ref.1, s32[2]{0:T(128)} %bitcast.1, bf16[1,4096,512]{2,1,0:T(8,128)(2,1)} %wq_ref.1, bf16[1,256,128]{2,1,0:T(8,128)(2,1)} %wk_ref.1, bf16[1,256,128]{2,1,0:T(8,128)(2,1)} %wv_ref.1, ...), custom_call_target="tpu_custom_call" | custom-call | tf_op jit(solution)/shard_map/pallas_call | solution.py:530
  23.1 0.8 %copy.13 = bf16[1,64,4096]{2,1,0:T(8,128)(2,1)} copy(bf16[1,64,4096]{2,1,0:T(8,128)(2,1)S(1)} %shard_map.100) | data formatting | bytes 1048576

commit v6 on v5

--- a/solution.py
+++ b/solution.py
@@ -116,6 +116,7 @@
     mixed,
     back,
     wkv,
+    image_v,
     img,
     part,
     part_out,
@@ -162,20 +163,21 @@
     def rows_of(index):
         return pl.ds(pl.multiple_of(index * depth, depth), depth)
 
+    own_rows = pl.ds(pl.multiple_of(core * image_rows, image_rows), image_rows)
+
+    def columns_of(index):
+        return pl.ds(pl.multiple_of(index * span, span), span)
+
     loads = [
         pltpu.make_async_copy(wk_ref.at[0], wkv.at[0, rows_of(spot), pl.ds(0, head)], load_sem.at[0]),
         pltpu.make_async_copy(wv_ref.at[0], wkv.at[0, rows_of(spot), pl.ds(head, head)], load_sem.at[1]),
-        pltpu.make_async_copy(
-            image_ref.at[core, :, pl.ds(pl.multiple_of(line * span, span), span)],
-            img.at[line, pl.ds(pl.multiple_of(core * image_rows, image_rows), image_rows)],
-            load_sem.at[2],
-        ),
-        pltpu.make_async_copy(text_ref.at[0], text_v.at[0], load_sem.at[3]),
-        pltpu.make_async_copy(wq_ref.at[0], wq_v, load_sem.at[4]),
-        pltpu.make_async_copy(wo_ref.at[0], wo_v.at[0], load_sem.at[5]),
-        pltpu.make_async_copy(qg_ref, query_gain, load_sem.at[6]),
-        pltpu.make_async_copy(kg_ref, key_gain, load_sem.at[7]),
-        pltpu.make_async_copy(start_ref, starts, load_sem.at[8]),
+        pltpu.make_async_copy(image_ref, image_v, load_sem.at[2]),
+        pltpu.make_async_copy(image_ref.at[core, :, columns_of(line)], img.at[line, own_rows], load_sem.at[3]),
+        pltpu.make_async_copy(qg_ref, query_gain, load_sem.at[4]),
+        pltpu.make_async_copy(kg_ref, key_gain, load_sem.at[5]),
+        pltpu.make_async_copy(start_ref, starts, load_sem.at[6]),
+        pltpu.make_async_copy(text_ref.at[0], text_v.at[0], load_sem.at[7]),
+        pltpu.make_async_copy(wq_ref.at[0], wq_v, load_sem.at[8]),
     ]
     for load in loads:
         load.start()
@@ -186,40 +188,40 @@
     peers += [(place, other)]
     for peer in peers:
         pl.semaphore_signal(barrier, inc=1, device_id=peer, device_id_type=MESH)
+    for load in loads[:3]:
+        load.wait()
     pl.semaphore_wait(barrier, len(peers))
 
-    image_copies = []
-    for distance in range(lines):
-        target = (line + distance) % lines
-        columns = pl.ds(pl.multiple_of(target * span, span), span)
-        for turn in range(2):
-            if distance == 0 and turn == 0:
-                continue
-            side = core if turn == 0 else other
-            copy = pltpu.make_async_remote_copy(
-                src_ref=image_ref.at[side, :, columns],
-                dst_ref=img.at[line, pl.ds(pl.multiple_of(core * image_rows, image_rows), image_rows)],
-                send_sem=i_send.at[distance, turn],
-                recv_sem=i_recv.at[distance, turn],
-                device_id=(line_peer(distance), side),
-                device_id_type=MESH,
-            )
+    weight_copies = [
+        pltpu.make_async_remote_copy(
+            src_ref=wkv.at[0, rows_of(spot)],
+            dst_ref=wkv.at[0, rows_of(spot)],
+            send_sem=w_send.at[distance],
+            recv_sem=w_recv.at[distance],
+            device_id=(quad_peer(distance), core),
+            device_id_type=MESH,
+        )
+        for distance in range(1, QUAD)
+    ]
+    image_copies = [
+        pltpu.make_async_remote_copy(
+            src_ref=image_v.at[side, :, columns_of((line + distance) % lines)],
+            dst_ref=img.at[line, own_rows],
+            send_sem=i_send.at[distance, turn],
+            recv_sem=i_recv.at[distance, turn],
+            device_id=(line_peer(distance), side),
+            device_id_type=MESH,
+        )
+        for distance in (*range(1, lines), 0)
+        for turn, side in enumerate((core, other))
+        if distance + turn > 0
+    ]
+    for i in range(QUAD - 1):
+        weight_copies[i].start()
+        for copy in image_copies[2 * i : 2 * i + 2]:
             copy.start()
-            image_copies.append(copy)
-
-    weight_copies = []
-    for distance in range(1, QUAD):
-        for which, ref in enumerate((wk_ref, wv_ref)):
-            copy = pltpu.make_async_remote_copy(
-                src_ref=ref.at[0],
-                dst_ref=wkv.at[0, rows_of(spot), pl.ds(which * head, head)],
-                send_sem=w_send.at[distance, which],
-                recv_sem=w_recv.at[distance, which],
-                device_id=(quad_peer(distance), core),
-                device_id_type=MESH,
-            )
-            copy.start()
-            weight_copies.append(copy)
+    for copy in image_copies[2 * QUAD - 2 :]:
+        copy.start()
 
     def across(src, dst, send, recv):
         return pltpu.make_async_remote_copy(
@@ -271,28 +273,33 @@
         rows = rows_of((spot + QUAD - distance) % QUAD)
         return across(wkv.at[0, rows], wkv.at[1, rows], relay_send.at[distance], relay_recv.at[distance])
 
-    loads[6].wait()
-    loads[7].wait()
+    loads[4].wait()
+    loads[5].wait()
     small[0, 0:1] = query_gain[...]
     small[0, 1:2] = key_gain[...]
     small[0, 2:3] = jnp.full((1, head), gate_ref[0], jnp.float32)
 
-    loads[0].wait()
-    loads[1].wait()
-
     small_copy.start()
+    middle = width // 2
+    out_loads = [
+        pltpu.make_async_copy(
+            wo_ref.at[0, :, pl.ds(i * middle, middle)], wo_v.at[0, :, pl.ds(i * middle, middle)], load_sem.at[9 + i]
+        )
+        for i in range(2)
+    ]
 
     @pl.when(core == 0)
     def _():
         text_copy.start()
         for piece in out_pieces[half:]:
             piece.start()
+        out_loads[0].start()
 
     @pl.when(core == 1)
     def _():
-        relay(0).start()
         for piece in query_pieces:
             piece.start()
+        relay(0).start()
 
     chunk = 512
 
@@ -317,8 +324,8 @@
         product = jnp.dot(left, right, preferred_element_type=jnp.float32)
         joint_sum[...] = product if i == 0 else joint_sum[...] + product
 
-    loads[3].wait()
-    loads[4].wait()
+    loads[7].wait()
+    loads[8].wait()
 
     def partial_sums(slot):
         groups = 2 * image_rows
@@ -340,7 +347,7 @@
         )
 
     def arrived():
-        loads[2].wait()
+        loads[3].wait()
         for copy in image_copies:
             copy.wait_recv()
 
@@ -357,7 +364,7 @@
             join(i, wo_v[0, :, at], wq_half[at, :])
 
         store_queries(project(1), 0)
-        loads[5].wait()
+        out_loads[0].wait()
         for i in range(half - 1):
             join_own(i)
         for copy in weight_copies:
@@ -385,11 +392,12 @@
         store_queries(sums[:tokens], 0)
         first[0] = sums[tokens:]
         first_copy.start()
+        for load in out_loads:
+            load.start()
         for i in range(half - 1):
             join_own(i)
         for distance in range(1, QUAD):
-            weight_copies[2 * distance - 2].wait_recv()
-            weight_copies[2 * distance - 1].wait_recv()
+            weight_copies[distance - 1].wait_recv()
             relay(distance).start()
         for piece in out_pieces[:half]:
             piece.start()
@@ -398,11 +406,12 @@
         join_own(half - 1)
         joint[0] = joint_sum[...].astype(jnp.bfloat16)
         joint_copy.start()
-        loads[5].wait()
+        for load in out_loads:
+            load.wait()
         small_copy.wait_recv()
 
     positions = lax.broadcasted_iota(jnp.int32, (tokens, 1), 0)
-    loads[8].wait()
+    loads[6].wait()
     seen = (positions >= starts[core]).astype(jnp.float32)
     seen_other = (positions >= starts[other]).astype(jnp.float32)
     root_size = math.sqrt(head)
@@ -543,6 +552,7 @@
             pltpu.VMEM((4, tokens, columns), jnp.bfloat16),
             pltpu.VMEM((tokens, width // 2), jnp.bfloat16),
             pltpu.VMEM((2, span, 2 * head), jnp.bfloat16),
+            pltpu.VMEM((2, image_rows, width), jnp.bfloat16),
             pltpu.VMEM((lines, groups, span), jnp.bfloat16),
             pltpu.VMEM((lines, 2, groups, 2 * head), jnp.float32),
             pltpu.VMEM((lines, 2, groups, 2 * head), jnp.bfloat16),
@@ -552,9 +562,9 @@
             pltpu.VMEM((1, head), jnp.float32),
             pltpu.VMEM((1, head), jnp.float32),
             pltpu.SMEM(image_start.shape[:1], jnp.int32),
-            dma((9,)),
-            dma((QUAD, 2)),
-            dma((QUAD, 2)),
+            dma((11,)),
+            dma((QUAD,)),
+            dma((QUAD,)),
             dma((lines, 2)),
             dma((lines, 2)),
             dma((QUAD,)),

time: 24.1 us -> 23.7 us (0.983)
  Pallas kernels: 22.5 us -> 22.1 us
    pallas_call x1, Pallas kernels: 22.5 us -> 22.1 us  [local_fused(): pl.pallas_call(functools.partial(kernel, lines), out_shape=jax.ShapeDtype...]
where the time goes in v6:
time: 23.7 us; the launch traced here: 23.6 us
  Pallas kernels  22.1 us (93%)
  local copies, waits for them, and re-layouts  0.8 us (3%)
  between operations  0.66 us (3%)
    pallas_call x1, Pallas kernels, local_fused(): pl.pallas_call(functools.partial(kernel, lines), out_shape=jax.ShapeDtype...  22.1 us
    unnamed x1, local copies, waits for them, and re-layouts  0.8 us

profile of v6, /device:TPU:0, one launch (start us, length us, event | category | flops | bytes accessed | tf_op | source)
XLA Modules:
  0.0 23.6 jit_solution(7382960106709430871)
XLA Ops:
  0.7 22.1 %shard_map.100 = bf16[1,64,4096]{2,1,0:T(8,128)(2,1)S(1)} custom-call(bf16[1,64,4096]{2,1,0:T(8,128)(2,1)} %text_ref.1, bf16[2,16,4096]{2,1,0:T(8,128)(2,1)} %image_ref.1, s32[2]{0:T(128)} %bitcast.1, bf16[1,4096,512]{2,1,0:T(8,128)(2,1)} %wq_ref.1, bf16[1,256,128]{2,1,0:T(8,128)(2,1)} %wk_ref.1, bf16[1,256,128]{2,1,0:T(8,128)(2,1)} %wv_ref.1, ...), custom_call_target="tpu_custom_call" | custom-call | tf_op jit(solution)/shard_map/pallas_call | solution.py:539
  22.8 0.8 %copy.13 = bf16[1,64,4096]{2,1,0:T(8,128)(2,1)} copy(bf16[1,64,4096]{2,1,0:T(8,128)(2,1)S(1)} %shard_map.100) | data formatting | bytes 1048576

commit v7 on v6

--- a/solution.py
+++ b/solution.py
@@ -244,6 +244,7 @@
         for i in range(PIECES)
     ]
     half = PIECES // 2
+    most = PIECES - 1
     query_pieces = [
         across(
             wq_ref.at[0, pl.ds(i * stretch, stretch)],
@@ -251,7 +252,7 @@
             big_send.at[1, i],
             big_recv.at[1, i],
         )
-        for i in range(half)
+        for i in range(most)
     ]
     small_copy = across(small.at[0], small.at[1], one_send.at[0], one_recv.at[0])
     text_copy = across(text_ref.at[0], text_v.at[1], one_send.at[1], one_recv.at[1])
@@ -280,26 +281,27 @@
     small[0, 2:3] = jnp.full((1, head), gate_ref[0], jnp.float32)
 
     small_copy.start()
-    middle = width // 2
     out_loads = [
         pltpu.make_async_copy(
-            wo_ref.at[0, :, pl.ds(i * middle, middle)], wo_v.at[0, :, pl.ds(i * middle, middle)], load_sem.at[9 + i]
-        )
-        for i in range(2)
+            wo_ref.at[0, :, pl.ds(i * stretch, stretch)], wo_v.at[0, :, pl.ds(i * stretch, stretch)], load_sem.at[9 + i]
+        )
+        for i in range(PIECES)
     ]
 
     @pl.when(core == 0)
     def _():
         text_copy.start()
-        for piece in out_pieces[half:]:
+        for piece in reversed(out_pieces[half:]):
             piece.start()
-        out_loads[0].start()
+        for load in out_loads[:most]:
+            load.start()
 
     @pl.when(core == 1)
     def _():
-        for piece in query_pieces:
+        query_pieces[0].start()
+        relay(0).start()
+        for piece in query_pieces[1:]:
             piece.start()
-        relay(0).start()
 
     chunk = 512
 
@@ -320,9 +322,8 @@
                 sums[:, h * head : (h + 1) * head], small[slot, 0:1]
             ).astype(jnp.bfloat16)
 
-    def join(i, left, right):
-        product = jnp.dot(left, right, preferred_element_type=jnp.float32)
-        joint_sum[...] = product if i == 0 else joint_sum[...] + product
+    def join(left, right):
+        return jnp.dot(left, right, preferred_element_type=jnp.float32)
 
     loads[7].wait()
     loads[8].wait()
@@ -359,14 +360,13 @@
     @pl.when(core == 0)
     def _():
         def join_own(i):
+            out_loads[i].wait()
             query_pieces[i].wait_recv()
             at = pl.ds(i * stretch, stretch)
-            join(i, wo_v[0, :, at], wq_half[at, :])
+            return join(wo_v[0, :, at], wq_half[at, :])
 
         store_queries(project(1), 0)
-        out_loads[0].wait()
-        for i in range(half - 1):
-            join_own(i)
+        joint_sum[...] = join_own(0)
         for copy in weight_copies:
             copy.wait_recv()
         arrived()
@@ -374,19 +374,15 @@
         for distance in range(QUAD):
             relay(distance).wait_recv()
         return_partials(1)
-        join_own(half - 1)
+        for i in range(1, most - 1):
+            joint_sum[...] += join_own(i)
+        joint_copy.wait_recv()
+        joint[0] = (joint_sum[...] + joint[1].astype(jnp.float32) + join_own(most - 1)).astype(jnp.bfloat16)
         small_copy.wait_recv()
         first_copy.wait_recv()
-        joint_copy.wait_recv()
-        joint[0] = (joint_sum[...] + joint[1].astype(jnp.float32)).astype(jnp.bfloat16)
 
     @pl.when(core == 1)
     def _():
-        def join_own(i):
-            out_pieces[half + i].wait_recv()
-            at = pl.ds((half + i) * stretch, stretch)
-            join(i, wo_v[1, :, at], wq_v[at, :])
-
         text_copy.wait_recv()
         sums = project(2)
         store_queries(sums[:tokens], 0)
@@ -394,8 +390,10 @@
         first_copy.start()
         for load in out_loads:
             load.start()
-        for i in range(half - 1):
-            join_own(i)
+        out_pieces[most].wait_recv()
+        at = pl.ds(most * stretch, stretch)
+        joint[0] = join(wo_v[1, :, at], wq_v[at, :]).astype(jnp.bfloat16)
+        joint_copy.start()
         for distance in range(1, QUAD):
             weight_copies[distance - 1].wait_recv()
             relay(distance).start()
@@ -403,9 +401,6 @@
             piece.start()
         arrived()
         return_partials(0)
-        join_own(half - 1)
-        joint[0] = joint_sum[...].astype(jnp.bfloat16)
-        joint_copy.start()
         for load in out_loads:
             load.wait()
         small_copy.wait_recv()
@@ -472,6 +467,8 @@
     @pl.when(core == 1)
     def _():
         advance(text_v.at[0], 0, attended, factor)
+        for piece in out_pieces[half:most]:
+            piece.wait_recv()
         mixed_copies[0].wait_recv()
         before = gate(1) * seen_other
         for i in range(PIECES):
@@ -544,7 +541,7 @@
         scratch_shapes=[
             pltpu.VMEM((2, tokens, width), jnp.bfloat16),
             pltpu.VMEM((width, columns), jnp.bfloat16),
-            pltpu.VMEM((width // 2, columns), jnp.bfloat16),
+            pltpu.VMEM((width - width // PIECES, columns), jnp.bfloat16),
             pltpu.VMEM((2, columns, width), jnp.bfloat16),
             pltpu.VMEM((columns, columns), jnp.float32),
             pltpu.VMEM((2, columns, columns), jnp.bfloat16),
@@ -562,7 +559,7 @@
             pltpu.VMEM((1, head), jnp.float32),
             pltpu.VMEM((1, head), jnp.float32),
             pltpu.SMEM(image_start.shape[:1], jnp.int32),
-            dma((11,)),
+            dma((9 + PIECES,)),
             dma((QUAD,)),
             dma((QUAD,)),
             dma((lines, 2)),

time: 23.7 us -> 23.1 us (0.975)
  Pallas kernels: 22.1 us -> 21.5 us
    pallas_call x1, Pallas kernels: 22.1 us -> 21.5 us  [local_fused(): pl.pallas_call(functools.partial(kernel, lines), out_shape=jax.ShapeDtype...]
where the time goes in v7:
time: 23.1 us; the launch traced here: 23 us
  Pallas kernels  21.5 us (93%)
  local copies, waits for them, and re-layouts  0.8 us (3%)
  between operations  0.66 us (3%)
    pallas_call x1, Pallas kernels, local_fused(): pl.pallas_call(functools.partial(kernel, lines), out_shape=jax.ShapeDtype...  21.5 us
    unnamed x1, local copies, waits for them, and re-layouts  0.8 us

profile of v7, /device:TPU:0, one launch (start us, length us, event | category | flops | bytes accessed | tf_op | source)
XLA Modules:
  0.0 23.0 jit_solution(15462689144799241841)
XLA Ops:
  0.7 21.5 %shard_map.100 = bf16[1,64,4096]{2,1,0:T(8,128)(2,1)S(1)} custom-call(bf16[1,64,4096]{2,1,0:T(8,128)(2,1)} %text_ref.1, bf16[2,16,4096]{2,1,0:T(8,128)(2,1)} %image_ref.1, s32[2]{0:T(128)} %bitcast.1, bf16[1,4096,512]{2,1,0:T(8,128)(2,1)} %wq_ref.1, bf16[1,256,128]{2,1,0:T(8,128)(2,1)} %wk_ref.1, bf16[1,256,128]{2,1,0:T(8,128)(2,1)} %wv_ref.1, ...), custom_call_target="tpu_custom_call" | custom-call | tf_op jit(solution)/shard_map/pallas_call | solution.py:536
  22.2 0.8 %copy.13 = bf16[1,64,4096]{2,1,0:T(8,128)(2,1)} copy(bf16[1,64,4096]{2,1,0:T(8,128)(2,1)S(1)} %shard_map.100) | data formatting | bytes 1048576

commit v8 on v7

--- a/solution.py
+++ b/solution.py
@@ -371,13 +371,12 @@
             copy.wait_recv()
         arrived()
         return_partials(0)
+        for i in range(1, most - 1):
+            joint_sum[...] += join_own(i)
         for distance in range(QUAD):
             relay(distance).wait_recv()
         return_partials(1)
-        for i in range(1, most - 1):
-            joint_sum[...] += join_own(i)
-        joint_copy.wait_recv()
-        joint[0] = (joint_sum[...] + joint[1].astype(jnp.float32) + join_own(most - 1)).astype(jnp.bfloat16)
+        joint[0] = (joint_sum[...] + join_own(most - 1)).astype(jnp.bfloat16)
         small_copy.wait_recv()
         first_copy.wait_recv()
 
@@ -390,10 +389,6 @@
         first_copy.start()
         for load in out_loads:
             load.start()
-        out_pieces[most].wait_recv()
-        at = pl.ds(most * stretch, stretch)
-        joint[0] = join(wo_v[1, :, at], wq_v[at, :]).astype(jnp.bfloat16)
-        joint_copy.start()
         for distance in range(1, QUAD):
             weight_copies[distance - 1].wait_recv()
             relay(distance).start()
@@ -401,6 +396,10 @@
             piece.start()
         arrived()
         return_partials(0)
+        out_pieces[most].wait_recv()
+        at = pl.ds(most * stretch, stretch)
+        joint[0] = join(wo_v[1, :, at], wq_v[at, :]).astype(jnp.bfloat16)
+        joint_copy.start()
         for load in out_loads:
             load.wait()
         small_copy.wait_recv()
@@ -453,6 +452,8 @@
         mixed[0] = attended
         mixed_copies[0].start()
         change = jnp.dot(attended, joint[0], preferred_element_type=jnp.float32)
+        joint_copy.wait_recv()
+        change += jnp.dot(attended, joint[1], preferred_element_type=jnp.float32)
         store_queries(first[1] + factor * change, 1)
         later = attend(1)
         mixed[1] = later

time: 23.1 us -> 23.3 us (level)
  no operation moved by 1% of the time
where the time goes in v8:
time: 23.3 us; the launch traced here: 23.1 us
  Pallas kernels  21.7 us (93%)
  local copies, waits for them, and re-layouts  0.8 us (3%)
  between operations  0.66 us (3%)
    pallas_call x1, Pallas kernels, local_fused(): pl.pallas_call(functools.partial(kernel, lines), out_shape=jax.ShapeDtype...  21.7 us
    unnamed x1, local copies, waits for them, and re-layouts  0.8 us

profile of v8, /device:TPU:0, one launch (start us, length us, event | category | flops | bytes accessed | tf_op | source)
XLA Modules:
  0.0 23.1 jit_solution(3826598417626607153)
XLA Ops:
  0.7 21.7 %shard_map.100 = bf16[1,64,4096]{2,1,0:T(8,128)(2,1)S(1)} custom-call(bf16[1,64,4096]{2,1,0:T(8,128)(2,1)} %text_ref.1, bf16[2,16,4096]{2,1,0:T(8,128)(2,1)} %image_ref.1, s32[2]{0:T(128)} %bitcast.1, bf16[1,4096,512]{2,1,0:T(8,128)(2,1)} %wq_ref.1, bf16[1,256,128]{2,1,0:T(8,128)(2,1)} %wk_ref.1, bf16[1,256,128]{2,1,0:T(8,128)(2,1)} %wv_ref.1, ...), custom_call_target="tpu_custom_call" | custom-call | tf_op jit(solution)/shard_map/pallas_call | solution.py:537
  22.3 0.8 %copy.13 = bf16[1,64,4096]{2,1,0:T(8,128)(2,1)} copy(bf16[1,64,4096]{2,1,0:T(8,128)(2,1)S(1)} %shard_map.100) | data formatting | bytes 1048576

commit v9 on v8

--- a/solution.py
+++ b/solution.py
@@ -126,6 +126,7 @@
     query_gain,
     key_gain,
     starts,
+    own_gate,
     load_sem,
     w_send,
     w_recv,
@@ -178,6 +179,7 @@
         pltpu.make_async_copy(start_ref, starts, load_sem.at[6]),
         pltpu.make_async_copy(text_ref.at[0], text_v.at[0], load_sem.at[7]),
         pltpu.make_async_copy(wq_ref.at[0], wq_v, load_sem.at[8]),
+        pltpu.make_async_copy(gate_ref, own_gate, load_sem.at[9]),
     ]
     for load in loads:
         load.start()
@@ -276,14 +278,15 @@
 
     loads[4].wait()
     loads[5].wait()
+    loads[9].wait()
     small[0, 0:1] = query_gain[...]
     small[0, 1:2] = key_gain[...]
-    small[0, 2:3] = jnp.full((1, head), gate_ref[0], jnp.float32)
+    small[0, 2:3] = own_gate[...]
 
     small_copy.start()
     out_loads = [
         pltpu.make_async_copy(
-            wo_ref.at[0, :, pl.ds(i * stretch, stretch)], wo_v.at[0, :, pl.ds(i * stretch, stretch)], load_sem.at[9 + i]
+            wo_ref.at[0, :, pl.ds(i * stretch, stretch)], wo_v.at[0, :, pl.ds(i * stretch, stretch)], load_sem.at[10 + i]
         )
         for i in range(PIECES)
     ]
@@ -303,7 +306,7 @@
         for piece in query_pieces[1:]:
             piece.start()
 
-    chunk = 512
+    chunk = 2048
 
     def project(slots):
         rows = slots * tokens
@@ -532,12 +535,11 @@
     groups = 2 * image_rows
     hbm = pl.BlockSpec(memory_space=pltpu.HBM)
     vmem = pl.BlockSpec(memory_space=pltpu.VMEM)
-    smem = pl.BlockSpec(memory_space=pltpu.SMEM)
     dma = pltpu.SemaphoreType.DMA
     return pl.pallas_call(
         functools.partial(kernel, lines),
         out_shape=jax.ShapeDtypeStruct((1, tokens, width), jnp.bfloat16),
-        in_specs=[hbm, hbm, hbm, hbm, hbm, hbm, hbm, hbm, hbm, smem],
+        in_specs=[hbm] * 10,
         out_specs=vmem,
         scratch_shapes=[
             pltpu.VMEM((2, tokens, width), jnp.bfloat16),
@@ -560,7 +562,8 @@
             pltpu.VMEM((1, head), jnp.float32),
             pltpu.VMEM((1, head), jnp.float32),
             pltpu.SMEM(image_start.shape[:1], jnp.int32),
-            dma((9 + PIECES,)),
+            pltpu.VMEM((1, head), jnp.float32),
+            dma((10 + PIECES,)),
             dma((QUAD,)),
             dma((QUAD,)),
             dma((lines, 2)),
@@ -589,7 +592,7 @@
         pltpu.with_memory_space_constraint(w_out, pltpu.HBM),
         pltpu.with_memory_space_constraint(query_gain, pltpu.HBM),
         pltpu.with_memory_space_constraint(key_gain, pltpu.HBM),
-        cross_gate,
+        pltpu.with_memory_space_constraint(jnp.broadcast_to(cross_gate[:, None], (1, head)), pltpu.HBM),
     )
 
 

time: 23.3 us -> 23.8 us (1.021)
  local copies, waits for them, and re-layouts: 0.8 us -> 1.39 us
    broadcast_in_dim x0 -> x1, local copies, waits for them, and re-layouts: none -> 0.59 us  [local_fused(): jnp.broadcast_to(cross_gate[:, None], (1, head))]
where the time goes in v9:
time: 23.8 us; the launch traced here: 23.7 us
  Pallas kernels  21.6 us (91%)
  local copies, waits for them, and re-layouts  1.39 us (6%)
  between operations  0.66 us (3%)
    pallas_call x1, Pallas kernels, local_fused(): pl.pallas_call(functools.partial(kernel, lines), out_shape=jax.ShapeDtype...  21.6 us
    unnamed x1, local copies, waits for them, and re-layouts  0.8 us
    broadcast_in_dim x1, local copies, waits for them, and re-layouts, local_fused(): jnp.broadcast_to(cross_gate[:, None], (1, head))  0.59 us

profile of v9, /device:TPU:0, one launch (start us, length us, event | category | flops | bytes accessed | tf_op | source)
XLA Modules:
  0.0 23.7 jit_solution(13410578807549898716)
XLA Ops:
  0.7 0.6 %broadcast_in_dim.9.gate_ref = f32[1,128]{1,0:T(1,128)} broadcast(f32[]{:T(128)} %bitcast.2), dimensions={} | broadcast | bytes 516 | tf_op jit(solution)/shard_map/broadcast_in_dim | solution.py:595
  1.2 21.6 %shard_map.100 = bf16[1,64,4096]{2,1,0:T(8,128)(2,1)S(1)} custom-call(bf16[1,64,4096]{2,1,0:T(8,128)(2,1)} %text_ref.1, bf16[2,16,4096]{2,1,0:T(8,128)(2,1)} %image_ref.1, s32[2]{0:T(128)} %bitcast.3, bf16[1,4096,512]{2,1,0:T(8,128)(2,1)} %wq_ref.1, bf16[1,256,128]{2,1,0:T(8,128)(2,1)} %wk_ref.1, bf16[1,256,128]{2,1,0:T(8,128)(2,1)} %wv_ref.1, ...), custom_call_target="tpu_custom_call" | custom-call | tf_op jit(solution)/shard_map/pallas_call | solution.py:539
  22.9 0.8 %copy.13 = bf16[1,64,4096]{2,1,0:T(8,128)(2,1)} copy(bf16[1,64,4096]{2,1,0:T(8,128)(2,1)S(1)} %shard_map.100) | data formatting | bytes 1048576

commit v10 on v8

--- a/solution.py
+++ b/solution.py
@@ -303,7 +303,7 @@
         for piece in query_pieces[1:]:
             piece.start()
 
-    chunk = 512
+    chunk = 2048
 
     def project(slots):
         rows = slots * tokens

time: 23.3 us -> 23.3 us (level)
  no operation moved by 1% of the time
where the time goes in v10:
time: 23.3 us; the launch traced here: 23.1 us
  Pallas kernels  21.7 us (93%)
  local copies, waits for them, and re-layouts  0.8 us (3%)
  between operations  0.66 us (3%)
    pallas_call x1, Pallas kernels, local_fused(): pl.pallas_call(functools.partial(kernel, lines), out_shape=jax.ShapeDtype...  21.7 us
    unnamed x1, local copies, waits for them, and re-layouts  0.8 us

profile of v10, /device:TPU:0, one launch (start us, length us, event | category | flops | bytes accessed | tf_op | source)
XLA Modules:
  0.0 23.1 jit_solution(15826510125704124358)
XLA Ops:
  0.7 21.7 %shard_map.100 = bf16[1,64,4096]{2,1,0:T(8,128)(2,1)S(1)} custom-call(bf16[1,64,4096]{2,1,0:T(8,128)(2,1)} %text_ref.1, bf16[2,16,4096]{2,1,0:T(8,128)(2,1)} %image_ref.1, s32[2]{0:T(128)} %bitcast.1, bf16[1,4096,512]{2,1,0:T(8,128)(2,1)} %wq_ref.1, bf16[1,256,128]{2,1,0:T(8,128)(2,1)} %wk_ref.1, bf16[1,256,128]{2,1,0:T(8,128)(2,1)} %wv_ref.1, ...), custom_call_target="tpu_custom_call" | custom-call | tf_op jit(solution)/shard_map/pallas_call | solution.py:537
  22.3 0.8 %copy.13 = bf16[1,64,4096]{2,1,0:T(8,128)(2,1)} copy(bf16[1,64,4096]{2,1,0:T(8,128)(2,1)S(1)} %shard_map.100) | data formatting | bytes 1048576
